TPU v7x, 128 devices: a whole 4x4x4 slice. The times are simulated.
128 devices in a mesh: case: 4 (over z_hi, core), gx: 8 (over y, z_lo), gy: 4 (over x).
Axes of the slice: x: 4, y: 4, z: 4 (z_hi: 2, z_lo: 2; z = z_hi * 2 + z_lo), core: 2. Of those that a mesh axis runs over, the one named last changes fastest.
Arguments:
- velocity: bfloat16 [4, 3, 128, 64, 128], P('case', None, 'gx', 'gy'), may hold values from -4 to 3
- target: bfloat16 [4, 3, 128, 64, 128], P('case', None, 'gx', 'gy'), may hold values from -3 to 3
- weight_in: bfloat16 [256, 12], replicated, may hold values from -1.75 to 1.75
- bias_in: float32 [256], replicated, may hold values from -3 to 3
- weight_mid: bfloat16 [256, 256], replicated, may hold values from -0.375 to 0.375
- bias_mid: float32 [256], replicated, may hold values from -3 to 3
- weight_out: bfloat16 [3, 256], replicated, may hold values from -0.375 to 0.375
- bias_out: float32 [3], replicated, may hold values from -3 to 3
- thrust_coef: float32 [100], replicated, may hold values from 0.5 to 1
- tile_cells: int32 [256, 128], P(('gx', 'gy')), may hold values from 0 to 32767
- tile_turbine: int32 [256], P(('gx', 'gy')), may hold values from -1 to 99, as said below
- tile_weight: float32 [256, 128], P(('gx', 'gy')), may hold values from 0.25 to 2
Outputs:
- velocity_new: bfloat16 [4, 3, 128, 64, 128], P('case', None, 'gx', 'gy')
- loss: float32 [], replicated
- step_weight_in: float32 [256, 12], replicated
- step_bias_in: float32 [256], replicated
- step_weight_mid: float32 [256, 256], replicated
- step_bias_mid: float32 [256], replicated
- step_weight_out: float32 [3, 256], replicated
- step_bias_out: float32 [3], replicated
- force_grad: bfloat16 [4, 3, 128, 64, 128], P('case', None, 'gx', 'gy')
Inputs may be any that keep to these rules, and one draw needn't show every extreme that they name: `tile_turbine`: in each device's block of 8 tile rows the used rows come first and the rest hold -1; in every draw some device has all 8 rows used.
All inputs are finite; a program needn't handle non-finite values.
Results may differ from a plain program's by a relative error of at most 0.0006.
The roundings to bfloat16 on the way count: a program that leaves them out, or rounds other values in their place, can miss the bound.
Values may be sent and summed in bfloat16 or wider, within the bound.
A program may use at most 128 MiB of HBM per device.

v0:
```python
import jax
import jax.numpy as jnp
from jax import lax
from jax.sharding import PartitionSpec as P

ITERS = 20


inflow = 1.0
step_dt = 0.4
viscosity = 0.1
epsilon_rms = 1e-06


def extended_2(block, sides, width):
    for axis, dim in sides:
        count = lax.axis_size(axis)
        forward = [(i, i + 1) for i in range(count - 1)]
        backward = [(target, source) for source, target in forward]
        low = lax.ppermute(
            lax.slice_in_dim(block, block.shape[dim] - width, None, axis=dim), axis, forward
        )
        high = lax.ppermute(lax.slice_in_dim(block, 0, width, axis=dim), axis, backward)
        block = jnp.concatenate([low, block, high], axis=dim)
    return block


def offset_view(extended, spatial_dim, offset):
    slicers = [slice(None)] * (extended.ndim - 3)
    for position in range(3):
        length = extended.shape[extended.ndim - 3 + position]
        if position == spatial_dim:
            slicers.append(slice(1 + offset, length - 1 + offset))
        else:
            slicers.append(slice(1, length - 1))
    return extended[tuple(slicers)]


def central(extended, spatial_dim):
    return 0.5 * (offset_view(extended, spatial_dim, 1) - offset_view(extended, spatial_dim, -1))


def neighbour_sum(extended):
    summed = offset_view(extended, 0, 1) + offset_view(extended, 0, -1)
    for spatial_dim in (1, 2):
        summed = (
            summed + offset_view(extended, spatial_dim, 1) + offset_view(extended, spatial_dim, -1)
        )
    return summed


def pad_depth(values, margin):
    padding = [(0, 0)] * (values.ndim - 1) + [(margin, margin)]
    return jnp.pad(values, padding)


def contract_cells(former, latter):
    return lax.dot_general(
        former, latter, (((1,), (1,)), ((), ())), preferred_element_type=jnp.float32
    )


def divergence_of(extended):
    return central(extended[0], 0) + central(extended[1], 1) + central(extended[2], 2)


def pressure_correction(divergence):
    source = divergence / step_dt

    def sweep(sweep_number, pressure):
        padded = extended_2(pressure, (("gx", 0), ("gy", 1)), 1)
        return (neighbour_sum(pad_depth(padded, 1)) - source) / 6.0

    pressure = lax.fori_loop(0, ITERS, sweep, jnp.zeros_like(source))
    padded = pad_depth(extended_2(pressure, (("gx", 0), ("gy", 1)), 1), 1)
    return step_dt * jnp.stack([central(padded, spatial_dim) for spatial_dim in range(3)])


def on_device(
    velocity,
    target,
    weight_in,
    bias_in,
    weight_mid,
    bias_mid,
    weight_out,
    bias_out,
    thrust_coef,
    tile_cells,
    tile_turbine,
    tile_weight,
):
    velocity_case = velocity[0]
    span_x = velocity_case.shape[1]
    span_y = velocity_case.shape[2]
    depth = velocity_case.shape[3]
    cells_dev = span_x * span_y * depth
    turbine_total = thrust_coef.shape[0]
    extended = extended_2(velocity_case, (("gx", 1), ("gy", 2)), 1)
    extended = pad_depth(extended, 1).astype(jnp.float32)
    gradients = [central(extended, spatial_dim) for spatial_dim in range(3)]
    fluctuation = velocity_case.astype(jnp.float32)
    full_speed = fluctuation.at[0].add(inflow)
    features = (
        jnp.concatenate(gradients + [fluctuation], 0).reshape(12, cells_dev).astype(jnp.bfloat16)
    )
    hidden_one = jnp.tanh(
        jnp.dot(weight_in, features, preferred_element_type=jnp.float32) + bias_in[:, None]
    ).astype(jnp.bfloat16)
    hidden_two = jnp.tanh(
        jnp.dot(weight_mid, hidden_one, preferred_element_type=jnp.float32) + bias_mid[:, None]
    ).astype(jnp.bfloat16)
    closure = (
        jnp.dot(weight_out, hidden_two, preferred_element_type=jnp.float32) + bias_out[:, None]
    )
    stream_flat = full_speed[0].reshape(cells_dev)
    sampled = stream_flat[tile_cells]
    weighted = jnp.sum(tile_weight * sampled, 1)
    weight_sums = jnp.sum(tile_weight, 1)
    matches = (tile_turbine[:, None] == jnp.arange(turbine_total, dtype=jnp.int32)[None, :]).astype(
        jnp.float32
    )
    disk_sum = jnp.sum(matches * weighted[:, None], 0)
    disk_area = jnp.sum(matches * weight_sums[:, None], 0)
    disk_sum, disk_area = lax.psum((disk_sum, disk_area), ("gx", "gy"))
    disk_speed = disk_sum / jnp.maximum(disk_area, 1.0)
    thrust = -0.5 * thrust_coef * disk_speed * jnp.abs(disk_speed)
    row_thrust = jnp.sum(matches * thrust[None, :], 1)
    spread = (tile_weight * row_thrust[:, None]).reshape(-1)
    turbine_force = jnp.zeros((cells_dev,), jnp.float32).at[tile_cells.reshape(-1)].add(spread)
    laplace = neighbour_sum(extended) - 6.0 * fluctuation
    advect = (
        full_speed[0] * gradients[0] + full_speed[1] * gradients[1] + full_speed[2] * gradients[2]
    )
    tendency = viscosity * laplace - advect + closure.reshape(3, span_x, span_y, depth)
    tendency = tendency.at[0].add(turbine_force.reshape(span_x, span_y, depth))
    provisional = (fluctuation + step_dt * tendency).astype(jnp.bfloat16)
    rim = pad_depth(extended_2(provisional, (("gx", 1), ("gy", 2)), 1), 1).astype(jnp.float32)
    updated = provisional.astype(jnp.float32) - pressure_correction(divergence_of(rim))
    velocity_new = updated.astype(jnp.bfloat16)
    mismatch = updated - target[0].astype(jnp.float32)
    cost_local = jnp.sum(mismatch * mismatch)
    seed_grad = 2.0 * mismatch
    rim_back = pad_depth(extended_2(seed_grad, (("gx", 1), ("gy", 2)), 1), 1)
    adjoint = seed_grad - pressure_correction(divergence_of(rim_back))
    force_field = (step_dt * adjoint).astype(jnp.bfloat16)
    force_grad = force_field.reshape(3, cells_dev)
    grad_weight_out = contract_cells(force_grad, hidden_two)
    grad_bias_out = jnp.sum(force_grad.astype(jnp.float32), 1)
    back_two = jnp.dot(weight_out.T, force_grad, preferred_element_type=jnp.float32)
    two_value = hidden_two.astype(jnp.float32)
    delta_two = (back_two * (1.0 - two_value * two_value)).astype(jnp.bfloat16)
    grad_bias_mid = jnp.sum(delta_two.astype(jnp.float32), 1)
    back_one = jnp.dot(weight_mid.T, delta_two, preferred_element_type=jnp.float32)
    one_value = hidden_one.astype(jnp.float32)
    delta_one = (back_one * (1.0 - one_value * one_value)).astype(jnp.bfloat16)
    grad_weight_in = contract_cells(delta_one, features)
    grad_bias_in = jnp.sum(delta_one.astype(jnp.float32), 1)
    grad_weight_mid = contract_cells(delta_two, hidden_one)
    summed = lax.psum(
        (
            grad_weight_in,
            grad_bias_in,
            grad_weight_mid,
            grad_bias_mid,
            grad_weight_out,
            grad_bias_out,
            cost_local,
        ),
        ("case", "gx", "gy"),
    )
    (
        grad_weight_in,
        grad_bias_in,
        grad_weight_mid,
        grad_bias_mid,
        grad_weight_out,
        grad_bias_out,
        cost,
    ) = summed
    totals = (
        grad_weight_in,
        grad_bias_in,
        grad_weight_mid,
        grad_bias_mid,
        grad_weight_out,
        grad_bias_out,
    )
    unit_count = weight_mid.shape[0]
    entry_total = (
        unit_count * weight_in.shape[1]
        + unit_count
        + unit_count * unit_count
        + unit_count
        + 3 * unit_count
        + 3
    )
    squares = sum((jnp.sum(grad_value * grad_value) for grad_value in totals))
    scale_rms = jnp.sqrt(squares / entry_total + epsilon_rms)
    cell_total = 3 * cells_dev * lax.axis_size("case") * lax.axis_size("gx") * lax.axis_size("gy")
    loss = cost / cell_total
    return (
        velocity_new[None],
        loss,
        totals[0] / scale_rms,
        totals[1] / scale_rms,
        totals[2] / scale_rms,
        totals[3] / scale_rms,
        totals[4] / scale_rms,
        totals[5] / scale_rms,
        force_field[None],
    )


def solution(mesh):
    placed = (
        P("case", None, "gx", "gy", None),
        P("case", None, "gx", "gy", None),
        P(),
        P(),
        P(),
        P(),
        P(),
        P(),
        P(),
        P(("gx", "gy"), None),
        P(("gx", "gy")),
        P(("gx", "gy"), None),
    )
    return jax.shard_map(
        on_device,
        mesh=mesh,
        in_specs=placed,
        out_specs=(
            P("case", None, "gx", "gy", None),
            P(),
            P(),
            P(),
            P(),
            P(),
            P(),
            P(),
            P("case", None, "gx", "gy", None),
        ),
        check_vma=False,
    )
```

profile of v0, /device:TPU:0, one launch (start us, length us, event | category | flops | bytes accessed | tf_op | source)
XLA Modules:
  0.0 1177.8 jit_solution(96007493584486095)
XLA Ops:
  14.9 6.2 gather_fusion
  21.3 84.1 %all-reduce.8 = (f32[100]{0:T(128)S(1)}, f32[100]{0:T(128)S(1)}) all-reduce(f32[100]{0:T(128)S(1)} %get-tuple-element.144, f32[100]{0:T(128)S(1)} %get-tuple-element.143), channel_id=1, replica_groups=mesh['case'=4,'gx'=8,'gy'=4] {'gx','gy'}, use_global_device_ids=true, to_apply=%region_2.3 | all-reduce | flops 200 | bytes 1600 | tf_op jit(solution)/shard_map/psum | solution.py:125
  108.4 6.1 scatter_custom_fusion
  116.7 8.5 fusion.14
  125.2 11.5 fusion.15
  136.8 10.2 fusion.19
  165.9 323.6 %while.28 = (s32[]{:T(128)}, f32[16,16,128]{2,1,0:T(8,128)S(1)}, f32[16,16,128]{2,1,0:T(8,128)S(1)}, s32[]{:T(128)}, s32[]{:T(128)}) while((s32[]{:T(128)}, f32[16,16,128]{2,1,0:T(8,128)S(1)}, f32[16,16,128]{2,1,0:T(8,128)S(1)}, s32[]{:T(128)}, s32[]{:T(128)}) %tuple.108), condition=%wide.region_9.10_spmd.clone, body=%wide.region_8.9_spmd.clone.sunk | while | flops 1038947 | bytes 1624839 | solution.py:74
  213.6 5.7 collective-permute-start.1
  229.9 5.7 collective-permute-start.1
  246.2 5.7 collective-permute-start.1
  262.5 5.7 collective-permute-start.1
  278.8 5.7 collective-permute-start.1
  295.1 5.7 collective-permute-start.1
  311.4 5.7 collective-permute-start.1
  327.7 5.7 collective-permute-start.1
  344.0 5.7 collective-permute-start.1
  360.3 5.8 collective-permute-start.1
  376.7 5.7 collective-permute-start.1
  393.0 5.7 collective-permute-start.1
  409.3 5.7 collective-permute-start.1
  425.7 5.7 collective-permute-start.1
  442.0 5.7 collective-permute-start.1
  458.3 5.7 collective-permute-start.1
  474.6 5.7 collective-permute-start.1
  534.6 324.7 %while.29 = (s32[]{:T(128)}, f32[16,16,128]{2,1,0:T(8,128)S(1)}, f32[16,16,128]{2,1,0:T(8,128)S(1)}, s32[]{:T(128)}, s32[]{:T(128)}) while((s32[]{:T(128)}, f32[16,16,128]{2,1,0:T(8,128)S(1)}, f32[16,16,128]{2,1,0:T(8,128)S(1)}, s32[]{:T(128)}, s32[]{:T(128)}) %tuple.111), condition=%wide.region_13.14_spmd.clone, body=%wide.region_12.13_spmd.clone.sunk | while | flops 1038947 | bytes 1624839 | solution.py:74
  567.0 5.7 collective-permute-start.5
  583.3 5.7 collective-permute-start.5
  599.6 5.7 collective-permute-start.5
  615.9 5.7 collective-permute-start.5
  632.2 5.7 collective-permute-start.5
  648.6 5.7 collective-permute-start.5
  664.9 5.7 collective-permute-start.5
  681.2 5.7 collective-permute-start.5
  697.5 5.7 collective-permute-start.5
  713.8 5.7 collective-permute-start.5
  730.1 5.7 collective-permute-start.5
  746.4 5.7 collective-permute-start.5
  762.7 5.8 collective-permute-start.5
  795.4 5.7 collective-permute-start.5
  811.7 5.7 collective-permute-start.5
  844.3 5.7 collective-permute-start.5
  881.6 8.1 fusion.33
  889.7 16.8 %convert_reduce_fusion = (f32[256]{0:T(256)S(1)}, bf16[32768,256]{1,0:T(8,128)(2,1)}) fusion(bf16[32768,256]{1,0:T(8,128)(2,1)} %fusion.15, bf16[3,256]{1,0:T(4,128)(2,1)S(1)} %copy-done.7, bf16[1,3,256,128]{3,2,1,0:T(8,128)(2,1)S(1)} %bitcast.97), kind=kOutput, calls=%fused_computation.65 | convolution fusion | flops 109051648 | bytes 33753600 | tf_op jit(solution)/shard_map/dot_general | solution.py:150
  906.5 15.8 %fusion.80 = f32[256,256]{1,0:T(8,128)} fusion(bf16[32768,256]{1,0:T(8,128)(2,1)} %get-tuple-element.218, bf16[32768,256]{1,0:T(8,128)(2,1)} %fusion.14), kind=kOutput, calls=%fused_computation.225 | convolution fusion | flops 4294967296 | bytes 33816576 | tf_op jit(solution)/shard_map/dot_general | solution.py:58
  922.2 20.1 %convert_reduce_fusion.1 = (f32[256]{0:T(256)S(1)}, bf16[32768,256]{1,0:T(8,128)(2,1)}) fusion(bf16[32768,256]{1,0:T(8,128)(2,1)} %fusion.14, bf16[32768,256]{1,0:T(8,128)(2,1)} %get-tuple-element.218, bf16[256,256]{1,0:T(8,128)(2,1)S(1)} %copy-done), kind=kOutput, calls=%fused_computation.66 | convolution fusion | flops 4353687552 | bytes 50463744 | tf_op jit(solution)/shard_map/dot_general | solution.py:154
  942.3 8.0 fusion.79
  950.4 69.1 %all-reduce.7 = (f32[]{:T(128)}, f32[256,12]{0,1:T(8,128)S(1)}, f32[256]{0:T(256)S(1)}, f32[256]{0:T(256)S(1)}, f32[3,256]{1,0:T(4,128)S(1)}, /*index=5*/f32[3]{0:T(128)S(1)}) all-reduce(f32[]{:T(128)} %get-tuple-element.185, f32[256,12]{0,1:T(8,128)S(1)} %fusion.79, ...), channel_id=1, replica_groups=mesh['case'=4,'gx'=8,'gy'=4] {'case','gx','gy'}, use_global_device_ids=true, to_apply=%region_11.12 | all-reduce | flops 4356 | bytes 34848 | tf_op jit(solution)/shard_map/psum | solution.py:160
  1024.4 136.6 %all-reduce.11.cloned.1.call-done = f32[256,256]{1,0:T(8,128)} async-done(((f32[256,256]{1,0:T(8,128)}), f32[256,256]{1,0:T(8,128)}) %all-reduce.11.cloned.1.call-update) | async-done | bytes 262160 | tf_op jit(solution)/shard_map/psum | solution.py:160
  (616 shorter events, 563.9 us)
Async XLA Ops:
  7.2 1153.8 %all-reduce.11.cloned.1.call-start = ((), (), s32[]{:S(2)}) async-start(), calls=%async_computation | async-start | bytes 524288 | tf_op jit(solution)/shard_map/psum | solution.py:160
  8.0 97.7 %collective-permute-start.8 = (bf16[3,1,16,128]{3,2,1,0:T(8,128)(2,1)S(1)}, bf16[3,1,16,128]{3,2,1,0:T(8,128)(2,1)S(1)}, u32[]{:S(2)}, u32[]{:S(2)}) collective-permute-start(bf16[3,1,16,128]{3,2,1,0:T(8,128)(2,1)S(1)} %get-tuple-element.201), channel_id=1, source_target_pairs={{0,4},{4,8},{8,12},{12,16},{16,20},{20,24},{24,28},{1,5},{5,9},{9,... | collective-permute-start | bytes 36872 | tf_op jit(solution)/shard_map/ppermute | solution.py:20
  11.9 93.8 %collective-permute-start.9 = (bf16[3,1,16,128]{3,2,1,0:T(8,128)(2,1)S(1)}, bf16[3,1,16,128]{3,2,1,0:T(8,128)(2,1)S(1)}, u32[]{:S(2)}, u32[]{:S(2)}) collective-permute-start(bf16[3,1,16,128]{3,2,1,0:T(8,128)(2,1)S(1)} %get-tuple-element.202), channel_id=1, source_target_pairs={{4,0},{8,4},{12,8},{16,12},{20,16},{24,20},{28,24},{5,1},{9,5},{13... | collective-permute-start | bytes 36872 | tf_op jit(solution)/shard_map/ppermute | solution.py:23
  105.8 8.8 collective-permute-start.10
  107.1 7.5 collective-permute-start.11
  212.3 7.0 collective-permute-start
  213.6 7.1 collective-permute-start.1
  228.6 7.0 collective-permute-start
  229.9 7.1 collective-permute-start.1
  244.9 7.0 collective-permute-start
  246.2 7.1 collective-permute-start.1
  262.5 7.1 collective-permute-start.1
  277.5 7.0 collective-permute-start
  278.8 7.1 collective-permute-start.1
  293.8 7.0 collective-permute-start
  295.1 7.1 collective-permute-start.1
  311.4 7.1 collective-permute-start.1
  326.4 7.0 collective-permute-start
  327.7 7.1 collective-permute-start.1
  344.0 7.1 collective-permute-start.1
  359.0 7.1 collective-permute-start
  360.3 7.1 collective-permute-start.1
  376.7 7.1 collective-permute-start.1
  393.0 7.1 collective-permute-start.1
  409.3 7.1 collective-permute-start.1
  425.7 7.1 collective-permute-start.1
  442.0 7.1 collective-permute-start.1
  458.3 7.1 collective-permute-start.1
  474.6 7.1 collective-permute-start.1
  567.0 7.1 collective-permute-start.5
  583.3 7.1 collective-permute-start.5
  599.6 7.1 collective-permute-start.5
  615.9 7.1 collective-permute-start.5
  632.2 7.1 collective-permute-start.5
  648.6 7.1 collective-permute-start.5
  664.9 7.1 collective-permute-start.5
  681.2 7.1 collective-permute-start.5
  697.5 7.1 collective-permute-start.5
  713.8 7.1 collective-permute-start.5
  730.1 7.1 collective-permute-start.5
  746.4 7.1 collective-permute-start.5
  761.4 7.1 collective-permute-start.4
  762.7 7.1 collective-permute-start.5
  779.1 7.1 collective-permute-start.5
  795.4 7.1 collective-permute-start.5
  811.7 7.1 collective-permute-start.5
  828.0 7.1 collective-permute-start.5
  844.3 7.1 collective-permute-start.5
  (146 other events, 1305.7 us)
Sparse Core Ops, SparseCore 0:
  1021.4 139.6 all-reduce.10
where the time goes:
time: 1180 us
  starting transfers between devices  572 us (48%)
  waiting for transfers between devices  281 us (24%)
  blocking collectives  153 us (13%)
  matrix products  99 us (8%)
  other arithmetic  39.8 us (3%)
  between operations  20.4 us (2%)
    ppermute x90, starting transfers between devices, extended_2(): lax.ppermute(lax.slice_in_dim(block, block.shape[dim] - width, None, axis...  456 us
    psum x1, waiting for transfers between devices, on_device(): lax.psum((grad_weight_in, grad_bias_in, grad_weight_mid, grad_bias_mid, g...  137 us
    ppermute x90, starting transfers between devices, extended_2(): lax.ppermute(lax.slice_in_dim(block, 0, width, axis=dim), axis, backward)  116 us
    ppermute x90, waiting for transfers between devices, extended_2(): lax.ppermute(lax.slice_in_dim(block, block.shape[dim] - width, None, axis...  108 us
    psum x1, blocking collectives, on_device(): disk_sum, disk_area = lax.psum((disk_sum, disk_area), ('gx', 'gy'))  84.1 us
    psum x1, blocking collectives, on_device(): lax.psum((grad_weight_in, grad_bias_in, grad_weight_mid, grad_bias_mid, g...  69.1 us
    ppermute x90, waiting for transfers between devices, extended_2(): lax.ppermute(lax.slice_in_dim(block, 0, width, axis=dim), axis, backward)  36.2 us
    dot_general x3, matrix products, contract_cells(): lax.dot_general(former, latter, (((1,), (1,)), ((), ())), preferred_eleme...  31.9 us
  transfers between devices with their start and end apart: 181, of which 95 were waited for; matrix products, arithmetic and copies ran while one was open for 1% of the time, Pallas kernels for 0%

commit v1 on v0

--- a/solution.py
+++ b/solution.py
@@ -1,15 +1,27 @@
+import functools
+import math
+
 import jax
 import jax.numpy as jnp
+import numpy as np
 from jax import lax
+from jax.experimental import pallas as pl
+from jax.experimental.pallas import tpu as pltpu
 from jax.sharding import PartitionSpec as P
 
 ITERS = 20
-
+MESH = pl.DeviceIdType.MESH
+HIGHEST = lax.Precision.HIGHEST
 
 inflow = 1.0
 step_dt = 0.4
 viscosity = 0.1
 epsilon_rms = 1e-06
+
+ROWS = 24
+LIVE = 18
+SLOTS = 32
+FIRST = 8
 
 
 def extended_2(block, sides, width):
@@ -60,20 +72,340 @@
     )
 
 
-def divergence_of(extended):
-    return central(extended[0], 0) + central(extended[1], 1) + central(extended[2], 2)
-
-
-def pressure_correction(divergence):
-    source = divergence / step_dt
-
-    def sweep(sweep_number, pressure):
-        padded = extended_2(pressure, (("gx", 0), ("gy", 1)), 1)
-        return (neighbour_sum(pad_depth(padded, 1)) - source) / 6.0
-
-    pressure = lax.fori_loop(0, ITERS, sweep, jnp.zeros_like(source))
-    padded = pad_depth(extended_2(pressure, (("gx", 0), ("gy", 1)), 1), 1)
-    return step_dt * jnp.stack([central(padded, spatial_dim) for spatial_dim in range(3)])
+def sines(count):
+    index = np.arange(1, count + 1, dtype=np.float64)
+    return math.sqrt(2.0 / (count + 1)) * np.sin(math.pi * np.outer(index, index) / (count + 1))
+
+
+def cosines(count):
+    return 2.0 * np.cos(math.pi * np.arange(1, count + 1, dtype=np.float64) / (count + 1))
+
+
+def solve_tables(n_gx, n_gy, span_x, span_y, depth):
+    nx, ny = n_gx * span_x, n_gy * span_y
+    group = n_gx * n_gy
+    modes = depth // group
+    base_x, base_y = sines(nx), sines(ny)
+    in_y = np.zeros((n_gy, modes, SLOTS, modes, ny))
+    for gy in range(n_gy):
+        for slot in range(FIRST - 1, FIRST + span_y + 1):
+            y = gy * span_y + slot - FIRST
+            if 0 <= y < ny:
+                for mode in range(modes):
+                    in_y[gy, mode, slot, mode] = base_y[y]
+    in_y = in_y.reshape(n_gy * modes * SLOTS, modes * ny)
+    in_x = np.zeros((nx, n_gx, ROWS))
+    for gx in range(n_gx):
+        for row in range(LIVE):
+            x = gx * span_x + (row if row < span_x else (-1 if row == span_x else span_x))
+            if 0 <= x < nx:
+                in_x[:, gx, row] = base_x[x]
+    in_x = in_x.reshape(nx, n_gx * ROWS)
+    plane = np.tile((cosines(nx)[:, None] + cosines(ny)[None, :]) / 6.0, (1, modes))
+    level = np.repeat((cosines(depth) / 6.0).reshape(modes, group).T, ny, axis=1)
+    tables = (sines(depth), in_y, in_y.T, in_x, in_x.T, plane, level[:, None, :])
+    return tuple(np.ascontiguousarray(table, dtype=np.float32) for table in tables)
+
+
+def dot_full(left, right):
+    return jnp.dot(left, right, precision=HIGHEST, preferred_element_type=jnp.float32)
+
+
+def depth_difference(values):
+    dim = values.ndim - 1
+    depth = values.shape[dim]
+    lane = lax.broadcasted_iota(jnp.int32, values.shape, dim)
+    above = jnp.where(lane == depth - 1, 0.0, pltpu.roll(values, depth - 1, dim))
+    below = jnp.where(lane == 0, 0.0, pltpu.roll(values, 1, dim))
+    return above - below
+
+
+def swap_groups(pieces, stride):
+    count = len(pieces)
+    lane = lax.broadcasted_iota(jnp.int32, pieces[0].shape, 1) // stride
+    results = []
+    for b in range(count):
+        result = None
+        for a in range(count):
+            shift = ((a - b) * stride) % (count * stride)
+            moved = pieces[a] if shift == 0 else pltpu.roll(pieces[a], shift, 1)
+            result = moved if result is None else jnp.where(lane == a, moved, result)
+        results.append(result)
+    return results
+
+
+def project_kernel(
+    n_gx,
+    n_gy,
+    u_ref,
+    t_ref,
+    base_z,
+    in_y,
+    out_y,
+    in_x,
+    out_x,
+    plane,
+    level,
+    new_ref,
+    force_ref,
+    cost_ref,
+    rext,
+    pext,
+    field,
+    gain,
+    send_a,
+    recv_a,
+    send_b,
+    recv_b,
+    send_sem,
+    recv_sem,
+):
+    case, gx, gy = lax.axis_index("case"), lax.axis_index("gx"), lax.axis_index("gy")
+    group = n_gx * n_gy
+    me = gy * n_gx + gx
+    span_x, span_y, depth = u_ref.shape[1:]
+    modes = depth // group
+
+    def device(index):
+        return (case, lax.rem(index, n_gx), index // n_gx)
+
+    for side in range(2):
+        recv_a[side, :, span_x:, :] = jnp.zeros((group, ROWS - span_x, depth), jnp.float32)
+
+    barrier = pltpu.get_barrier_semaphore()
+
+    def greet(step, carry):
+        pl.semaphore_signal(
+            barrier,
+            inc=1,
+            device_id=device(lax.rem(me + step, group)),
+            device_id_type=MESH,
+        )
+        return carry
+
+    lax.fori_loop(1, group, greet, 0)
+
+    ratio = plane[...] + level[me]
+    total = jnp.ones_like(ratio)
+    for _ in range(ITERS - 1):
+        total = total * ratio + 1.0
+    gain[...] = total * (-1.0 / 24.0)
+    rext[...] = jnp.zeros_like(rext)
+
+    def exchange(number, outgoing, incoming):
+        def start(step, carry):
+            peer = lax.rem(me + step, group)
+            pltpu.make_async_remote_copy(
+                src_ref=outgoing.at[peer, pl.ds(0, LIVE)],
+                dst_ref=incoming.at[me, pl.ds(0, LIVE)],
+                send_sem=send_sem.at[number],
+                recv_sem=recv_sem.at[number],
+                device_id=device(peer),
+                device_id_type=MESH,
+            ).start()
+            return carry
+
+        lax.fori_loop(1, group, start, 0)
+        incoming[me, pl.ds(0, LIVE)] = outgoing[me, pl.ds(0, LIVE)]
+        landed = incoming.at[pl.ds(0, group - 1), pl.ds(0, LIVE)]
+        pltpu.make_async_copy(landed, landed, recv_sem.at[number]).wait()
+
+    def sent(number, outgoing):
+        left = outgoing.at[pl.ds(0, group - 1), pl.ds(0, LIVE)]
+        pltpu.make_async_copy(left, left, send_sem.at[number]).wait()
+
+    def solve(number, q_x, q_y, q_z):
+        zero_x = jnp.zeros((1, span_y, depth), jnp.float32)
+        inner = jnp.concatenate([q_x[1:], zero_x], 0) - jnp.concatenate([zero_x, q_x[:-1]], 0)
+        inner = inner + depth_difference(q_z)
+        last = FIRST + span_y
+        wide = jnp.concatenate(
+            [
+                jnp.zeros((span_x, FIRST, depth), jnp.float32),
+                q_y,
+                jnp.zeros((span_x, SLOTS - last, depth), jnp.float32),
+            ],
+            1,
+        )
+        rext[0:span_x] = pltpu.roll(wide, SLOTS - 1, 1) - pltpu.roll(wide, 1, 1)
+        rext[0:span_x, FIRST:last, :] = rext[0:span_x, FIRST:last, :] + inner
+        rext[span_x, FIRST:last, :] = q_x[0]
+        rext[span_x + 1, FIRST:last, :] = -q_x[span_x - 1]
+        if number > 0:
+            sent(2 * number - 2, send_a)
+        for part in range(rext.shape[0] // modes):
+            cells = rext[part * modes : (part + 1) * modes].reshape(modes * SLOTS, depth)
+            turned = dot_full(cells, base_z[...]).T
+            pieces = [turned[m * group : (m + 1) * group] for m in range(modes)]
+            for inside, piece in enumerate(swap_groups(pieces, SLOTS)):
+                if part * modes + inside < LIVE:
+                    send_a[:, part * modes + inside, :] = piece
+        if number == 0:
+            pl.semaphore_wait(barrier, group - 1)
+        arrived = recv_a.at[number]
+        exchange(2 * number, send_a, arrived)
+        along_y = None
+        for block in range(n_gy):
+            rows = arrived[block * n_gx : (block + 1) * n_gx].reshape(n_gx * ROWS, depth)
+            part = dot_full(rows, in_y[block * depth : (block + 1) * depth, :])
+            along_y = part if along_y is None else along_y + part
+        spectrum = dot_full(in_x[...], along_y) * gain[...]
+        back = dot_full(out_x[...], spectrum)
+        if number > 0:
+            sent(2 * number - 1, send_b)
+        for block in range(n_gy):
+            part = dot_full(back, out_y[:, block * depth : (block + 1) * depth])
+            send_b[block * n_gx : (block + 1) * n_gx] = part.reshape(n_gx, ROWS, depth)
+        arrived = recv_b.at[number]
+        exchange(2 * number + 1, send_b, arrived)
+        for part in range(pext.shape[0] // modes):
+            pieces = [
+                arrived[:, min(part * modes + inside, LIVE - 1), :] for inside in range(modes)
+            ]
+            turned = jnp.concatenate(swap_groups(pieces, SLOTS), 0).T
+            pext[part * modes : (part + 1) * modes] = dot_full(turned, base_z[...]).reshape(
+                modes, SLOTS, depth
+            )
+
+    def slope():
+        last = FIRST + span_y
+        middle = pext[0:span_x, FIRST:last, :]
+        low = pext[span_x : span_x + 1, FIRST:last, :]
+        high = pext[span_x + 1 : span_x + 2, FIRST:last, :]
+        along_x = jnp.concatenate([middle[1:], high], 0) - jnp.concatenate([low, middle[:-1]], 0)
+        along_y = (
+            pext[0:span_x, FIRST + 1 : last + 1, :] - pext[0:span_x, FIRST - 1 : last - 1, :]
+        )
+        return along_x, along_y, depth_difference(middle)
+
+    solve(0, *[u_ref[component].astype(jnp.float32) for component in range(3)])
+    cost = jnp.zeros((8, depth), jnp.float32)
+    for component, change in enumerate(slope()):
+        updated = u_ref[component].astype(jnp.float32) - change
+        new_ref[component] = updated.astype(jnp.bfloat16)
+        mismatch = updated - t_ref[component].astype(jnp.float32)
+        cost = cost + jnp.sum((mismatch * mismatch).reshape(-1, 8, depth), 0)
+        field[component] = 2.0 * mismatch
+    cost_ref[...] = cost
+    solve(1, field[0], field[1], field[2])
+    for component, change in enumerate(slope()):
+        force_ref[component] = (step_dt * (field[component] - change)).astype(jnp.bfloat16)
+    sent(2, send_a)
+    sent(3, send_b)
+
+
+def project(provisional, target):
+    n_gx, n_gy = lax.axis_size("gx"), lax.axis_size("gy")
+    group = n_gx * n_gy
+    _, span_x, span_y, depth = provisional.shape
+    tables = solve_tables(n_gx, n_gy, span_x, span_y, depth)
+    f32 = jnp.float32
+    vmem = pl.BlockSpec(memory_space=pltpu.VMEM)
+    return pl.pallas_call(
+        functools.partial(project_kernel, n_gx, n_gy),
+        out_shape=(
+            jax.ShapeDtypeStruct(provisional.shape, jnp.bfloat16),
+            jax.ShapeDtypeStruct(provisional.shape, jnp.bfloat16),
+            jax.ShapeDtypeStruct((8, depth), f32),
+        ),
+        in_specs=[vmem] * (2 + len(tables)),
+        out_specs=(vmem, vmem, vmem),
+        scratch_shapes=[
+            pltpu.VMEM((span_x + 4, SLOTS, depth), f32),
+            pltpu.VMEM((span_x + 4, SLOTS, depth), f32),
+            pltpu.VMEM((3, span_x, span_y, depth), f32),
+            pltpu.VMEM(tables[5].shape, f32),
+            pltpu.VMEM((group, ROWS, depth), f32),
+            pltpu.VMEM((2, group, ROWS, depth), f32),
+            pltpu.VMEM((group, ROWS, depth), f32),
+            pltpu.VMEM((2, group, ROWS, depth), f32),
+            pltpu.SemaphoreType.DMA((4,)),
+            pltpu.SemaphoreType.DMA((4,)),
+        ],
+        compiler_params=pltpu.CompilerParams(
+            collective_id=0, has_side_effects=True, vmem_limit_bytes=48 * 1024 * 1024
+        ),
+        name="project",
+    )(provisional, target, *tables)
+
+
+def reduce_kernel(sizes, part_ref, out_ref, recv, mine, send_sem, recv_sem):
+    n_case, n_gx, n_gy = sizes
+    total = n_case * n_gx * n_gy
+    case, gx, gy = lax.axis_index("case"), lax.axis_index("gx"), lax.axis_index("gy")
+    me = (case * n_gx + gx) * n_gy + gy
+
+    def device(index):
+        return (index // (n_gx * n_gy), lax.rem(index // n_gy, n_gx), lax.rem(index, n_gy))
+
+    barrier = pltpu.get_barrier_semaphore()
+
+    def greet(step, carry):
+        pl.semaphore_signal(
+            barrier, inc=1, device_id=device(lax.rem(me + step, total)), device_id_type=MESH
+        )
+        return carry
+
+    lax.fori_loop(1, total, greet, 0)
+    pl.semaphore_wait(barrier, total - 1)
+
+    def scatter(step, carry):
+        peer = lax.rem(me + step, total)
+        pltpu.make_async_remote_copy(
+            src_ref=part_ref.at[peer],
+            dst_ref=recv.at[me],
+            send_sem=send_sem.at[0],
+            recv_sem=recv_sem.at[0],
+            device_id=device(peer),
+            device_id_type=MESH,
+        ).start()
+        return carry
+
+    lax.fori_loop(1, total, scatter, 0)
+    recv[me] = part_ref[me]
+    others = recv.at[pl.ds(0, total - 1)]
+    pltpu.make_async_copy(others, others, recv_sem.at[0]).wait()
+    mine[...] = jnp.sum(recv[...], 0)
+
+    def spread(step, carry):
+        peer = lax.rem(me + step, total)
+        pltpu.make_async_remote_copy(
+            src_ref=mine,
+            dst_ref=out_ref.at[me],
+            send_sem=send_sem.at[1],
+            recv_sem=recv_sem.at[1],
+            device_id=device(peer),
+            device_id_type=MESH,
+        ).start()
+        return carry
+
+    lax.fori_loop(1, total, spread, 0)
+    out_ref[me] = mine[...]
+    others = out_ref.at[pl.ds(0, total - 1)]
+    pltpu.make_async_copy(others, others, recv_sem.at[1]).wait()
+    pltpu.make_async_copy(others, others, send_sem.at[0]).wait()
+    pltpu.make_async_copy(others, others, send_sem.at[1]).wait()
+
+
+def reduce_all(parts):
+    sizes = (lax.axis_size("case"), lax.axis_size("gx"), lax.axis_size("gy"))
+    vmem = pl.BlockSpec(memory_space=pltpu.VMEM)
+    return pl.pallas_call(
+        functools.partial(reduce_kernel, sizes),
+        out_shape=jax.ShapeDtypeStruct(parts.shape, jnp.float32),
+        in_specs=[vmem],
+        out_specs=vmem,
+        scratch_shapes=[
+            pltpu.VMEM(parts.shape, jnp.float32),
+            pltpu.VMEM(parts.shape[1:], jnp.float32),
+            pltpu.SemaphoreType.DMA((2,)),
+            pltpu.SemaphoreType.DMA((2,)),
+        ],
+        compiler_params=pltpu.CompilerParams(
+            collective_id=1, has_side_effects=True, vmem_limit_bytes=16 * 1024 * 1024
+        ),
+        name="reduce_all",
+    )(parts)
 
 
 def on_device(
@@ -135,15 +467,7 @@
     tendency = viscosity * laplace - advect + closure.reshape(3, span_x, span_y, depth)
     tendency = tendency.at[0].add(turbine_force.reshape(span_x, span_y, depth))
     provisional = (fluctuation + step_dt * tendency).astype(jnp.bfloat16)
-    rim = pad_depth(extended_2(provisional, (("gx", 1), ("gy", 2)), 1), 1).astype(jnp.float32)
-    updated = provisional.astype(jnp.float32) - pressure_correction(divergence_of(rim))
-    velocity_new = updated.astype(jnp.bfloat16)
-    mismatch = updated - target[0].astype(jnp.float32)
-    cost_local = jnp.sum(mismatch * mismatch)
-    seed_grad = 2.0 * mismatch
-    rim_back = pad_depth(extended_2(seed_grad, (("gx", 1), ("gy", 2)), 1), 1)
-    adjoint = seed_grad - pressure_correction(divergence_of(rim_back))
-    force_field = (step_dt * adjoint).astype(jnp.bfloat16)
+    velocity_new, force_field, cost_parts = project(provisional, target[0])
     force_grad = force_field.reshape(3, cells_dev)
     grad_weight_out = contract_cells(force_grad, hidden_two)
     grad_bias_out = jnp.sum(force_grad.astype(jnp.float32), 1)
@@ -157,57 +481,43 @@
     grad_weight_in = contract_cells(delta_one, features)
     grad_bias_in = jnp.sum(delta_one.astype(jnp.float32), 1)
     grad_weight_mid = contract_cells(delta_two, hidden_one)
-    summed = lax.psum(
-        (
-            grad_weight_in,
+    devices = lax.axis_size("case") * lax.axis_size("gx") * lax.axis_size("gy")
+    units = weight_mid.shape[0]
+    small = jnp.concatenate(
+        [
+            grad_weight_in.reshape(-1),
             grad_bias_in,
-            grad_weight_mid,
             grad_bias_mid,
-            grad_weight_out,
+            grad_weight_out.reshape(-1),
             grad_bias_out,
-            cost_local,
-        ),
-        ("case", "gx", "gy"),
-    )
-    (
-        grad_weight_in,
-        grad_bias_in,
-        grad_weight_mid,
-        grad_bias_mid,
-        grad_weight_out,
-        grad_bias_out,
-        cost,
-    ) = summed
-    totals = (
-        grad_weight_in,
-        grad_bias_in,
-        grad_weight_mid,
-        grad_bias_mid,
-        grad_weight_out,
-        grad_bias_out,
-    )
-    unit_count = weight_mid.shape[0]
-    entry_total = (
-        unit_count * weight_in.shape[1]
-        + unit_count
-        + unit_count * unit_count
-        + unit_count
-        + 3 * unit_count
-        + 3
-    )
-    squares = sum((jnp.sum(grad_value * grad_value) for grad_value in totals))
+            jnp.sum(cost_parts)[None],
+        ]
+    )
+    small_count = small.shape[0]
+    small = jnp.pad(small, (0, devices * 128 - small_count)).reshape(devices, 1, 128)
+    parts = jnp.concatenate([grad_weight_mid.reshape(devices, -1, 128), small], 1)
+    summed = reduce_all(parts)
+    big = summed[:, :-1].reshape(units, units)
+    small = summed[:, -1].reshape(-1)[:small_count]
+    cost = small[-1]
+    small = small[:-1]
+    entry_total = units * units + small.shape[0]
+    squares = jnp.sum(big * big) + jnp.sum(small * small)
     scale_rms = jnp.sqrt(squares / entry_total + epsilon_rms)
-    cell_total = 3 * cells_dev * lax.axis_size("case") * lax.axis_size("gx") * lax.axis_size("gy")
-    loss = cost / cell_total
+    big = big / scale_rms
+    small = small / scale_rms
+    bounds = np.cumsum([units * weight_in.shape[1], units, units, 3 * units])
+    first, second, third, fourth, fifth = jnp.split(small, bounds)
+    loss = cost / (3 * cells_dev * devices)
     return (
         velocity_new[None],
         loss,
-        totals[0] / scale_rms,
-        totals[1] / scale_rms,
-        totals[2] / scale_rms,
-        totals[3] / scale_rms,
-        totals[4] / scale_rms,
-        totals[5] / scale_rms,
+        first.reshape(weight_in.shape),
+        second,
+        big,
+        third,
+        fourth.reshape(weight_out.shape),
+        fifth,
         force_field[None],
     )
 

time: 1180 us -> 294 us (0.25)
  starting transfers between devices: 572 us -> 7.77 us
  waiting for transfers between devices: 281 us -> 0.01 us
  blocking collectives: 153 us -> 84.1 us
  Pallas kernels: 0 us -> 64.7 us
  other arithmetic: 39.8 us -> 19.2 us
  between operations: 20.4 us -> 4.15 us
    ppermute x90 -> x2, starting transfers between devices: 456 us -> 5.18 us  [extended_2(): lax.ppermute(lax.slice_in_dim(block, block.shape[dim] - width, None, axis...]
    psum x1 -> x0, waiting for transfers between devices: 137 us -> none  [on_device(): lax.psum((grad_weight_in, grad_bias_in, grad_weight_mid, grad_bias_mid, g...]
    ppermute x90 -> x2, starting transfers between devices: 116 us -> 2.58 us  [extended_2(): lax.ppermute(lax.slice_in_dim(block, 0, width, axis=dim), axis, backward)]
    ppermute x90 -> x2, waiting for transfers between devices: 108 us -> 0.01 us  [extended_2(): lax.ppermute(lax.slice_in_dim(block, block.shape[dim] - width, None, axis...]
    psum x1 -> x0, blocking collectives: 69.1 us -> none  [on_device(): lax.psum((grad_weight_in, grad_bias_in, grad_weight_mid, grad_bias_mid, g...]
    pallas_call x0 -> x2, Pallas kernels: none -> 64.7 us  [the longest x1 40.7 us: project(): pl.pallas_call(functools.partial(project_kernel, n_gx, n_gy), out_shape=(...]
    ppermute x90 -> x2, waiting for transfers between devices: 36.2 us -> 0.01 us  [extended_2(): lax.ppermute(lax.slice_in_dim(block, 0, width, axis=dim), axis, backward)]
    concatenate x83 -> x1, other arithmetic: 12.2 us -> 0.11 us  [on_device(): jnp.concatenate([grad_weight_mid.reshape(devices, -1, 128), small], 1)]
  transfers between devices with their start and end apart: 181 -> 4, of which waited for: 95 -> 0; matrix products, arithmetic and copies ran while one was open for 1% -> 6% of each run, Pallas kernels for 0% -> 0%
where the time goes in v1:
time: 294 us; the launch traced here: 292 us
  matrix products  98.2 us (33%)
  blocking collectives  84.1 us (29%)
  Pallas kernels  64.7 us (22%)
  other arithmetic  19.2 us (7%)
  local copies, waits for them, and re-layouts  14.2 us (5%)
  starting transfers between devices  7.77 us (3%)
  between operations  4.15 us (1%)
    psum x1, blocking collectives, on_device(): disk_sum, disk_area = lax.psum((disk_sum, disk_area), ('gx', 'gy'))  84.1 us
    pallas_call x1, Pallas kernels, project(): pl.pallas_call(functools.partial(project_kernel, n_gx, n_gy), out_shape=(...  40.7 us
    dot_general x3, matrix products, contract_cells(): lax.dot_general(former, latter, (((1,), (1,)), ((), ())), preferred_eleme...  30.2 us
    pallas_call x1, Pallas kernels, reduce_all(): pl.pallas_call(functools.partial(reduce_kernel, sizes), out_shape=jax.Sha...  24 us
    dot_general x1, matrix products, on_device(): jnp.dot(weight_mid.T, delta_two, preferred_element_type=jnp.float32)  20 us
    dot_general x1, matrix products, on_device(): jnp.dot(weight_out.T, force_grad, preferred_element_type=jnp.float32)  16.8 us
    dot_general x1, matrix products, on_device(): jnp.dot(weight_mid, hidden_one, preferred_element_type=jnp.float32)  11.5 us
    dot_general x1, matrix products, on_device(): jnp.dot(weight_out, hidden_two, preferred_element_type=jnp.float32)  10.3 us
  transfers between devices with their start and end apart: 4, of which 0 were waited for; matrix products, arithmetic and copies ran while one was open for 6% of the time, Pallas kernels for 0%

profile of v1, /device:TPU:0, one launch (start us, length us, event | category | flops | bytes accessed | tf_op | source)
XLA Modules:
  0.0 292.3 jit_solution(11499653313374784592)
XLA Ops:
  0.7 0.8 fusion.28
  1.4 3.9 %collective-permute-start = (bf16[3,1,16,128]{3,2,1,0:T(8,128)(2,1)S(1)}, bf16[3,1,16,128]{3,2,1,0:T(8,128)(2,1)S(1)}, u32[]{:S(2)}, u32[]{:S(2)}) collective-permute-start(bf16[3,1,16,128]{3,2,1,0:T(8,128)(2,1)S(1)} %get-tuple-element.72), channel_id=1, source_target_pairs={{0,4},{4,8},{8,12},{12,16},{16,20},{20,24},{24,28},{1,5},{5,9},{9,... | collective-permute-start | bytes 36872 | tf_op jit(solution)/shard_map/ppermute | solution.py:32
  5.3 1.3 collective-permute-start.1
  6.6 1.0 bitcast_convert_fusion
  7.6 0.7 fusion.25
  8.3 6.2 %gather_fusion = f32[1024]{0:T(1024)S(1)} fusion(f32[32768]{0:T(1024)S(1)} %bitcast.68, s32[1024]{0:T(1024)S(1)} %fusion.25), kind=kCustom, calls=%fused_computation | custom fusion | bytes 12288 | tf_op jit(solution)/shard_map/gather | solution.py:449
  14.5 0.8 fusion.27
  15.3 0.8 select_reduce_fusion.1
  16.1 84.1 %all-reduce.2 = (f32[100]{0:T(128)S(1)}, f32[100]{0:T(128)S(1)}) all-reduce(f32[100]{0:T(128)S(1)} %get-tuple-element.60, f32[100]{0:T(128)S(1)} %get-tuple-element.59), channel_id=1, replica_groups=mesh['case'=4,'gx'=8,'gy'=4] {'gx','gy'}, use_global_device_ids=true, to_apply=%region_2.3 | all-reduce | flops 200 | bytes 1600 | tf_op jit(solution)/shard_map/psum | solution.py:457
  100.2 0.7 abs_multiply_fusion
  100.8 0.8 select_reduce_fusion
  101.7 0.8 multiply_bitcast_fusion.1
  102.4 1.0 pad_maximum_fusion.4
  103.4 1.3 collective-permute-start.2
  104.7 1.3 collective-permute-start.3
  106.0 0.7 compare_select_fusion
  106.7 6.0 %scatter_custom_fusion = f32[32768]{0:T(1024)S(1)} fusion(s32[1024]{0:T(1024)S(1)} %bitcast.84, f32[1024]{0:T(1024)S(1)} %multiply_bitcast_fusion.1, f32[]{:T(128)} %constant.91.clone.1), kind=kCustom, calls=%fused_computation.53 | custom fusion | flops 1024 | bytes 131076 | tf_op jit(solution)/shard_map/scatter-add | solution.py:462
  112.7 1.5 fusion.8
  114.2 0.6 multiply_convert_fusion.2
  114.8 1.0 pad_maximum_fusion
  115.9 0.7 copy.33
  116.6 9.4 %fusion.2 = bf16[32768,256]{1,0:T(8,128)(2,1)} fusion(bf16[12,32768]{1,0:T(8,128)(2,1)S(1)} %bitcast.76, bf16[256,12]{0,1:T(8,128)(2,1)} %param.25, f32[256]{0:T(256)} %param.26), kind=kOutput, calls=%fused_computation.8 | convolution fusion | flops 218103808 | bytes 17570816 | tf_op jit(solution)/shard_map/dot_general | solution.py:440
  126.0 11.5 %fusion.3 = bf16[32768,256]{1,0:T(8,128)(2,1)} fusion(bf16[32768,256]{1,0:T(8,128)(2,1)} %fusion.2, bf16[256,256]{1,0:T(8,128)(2,1)S(1)} %copy-done, f32[256]{0:T(256)S(1)} %copy-done.12), kind=kOutput, calls=%fused_computation.9 | convolution fusion | flops 4311744512 | bytes 33686528 | tf_op jit(solution)/shard_map/dot_general | solution.py:443
  137.6 10.3 %fusion.7 = f32[1,3,256,128]{3,1,2,0:T(4,128)S(1)} fusion(bf16[32768,256]{1,0:T(8,128)(2,1)} %fusion.3, bf16[3,256]{1,0:T(4,128)(2,1)S(1)} %copy-done.11, f32[3]{0:T(128)S(1)} %copy-done.10), kind=kOutput, calls=%fused_computation.18 | convolution fusion | flops 50429952 | bytes 17171980 | tf_op jit(solution)/shard_map/dot_general | solution.py:446
  148.0 0.6 subtract_add_fusion
  148.8 40.7 %project.1 = (bf16[3,16,16,128]{3,2,1,0:T(8,128)(2,1)S(1)}, bf16[3,16,16,128]{3,2,1,0:T(8,128)(2,1)S(1)}, f32[8,128]{1,0:T(8,128)S(1)}) custom-call(bf16[3,16,16,128]{3,2,1,0:T(8,128)(2,1)S(1)} %add_convert_fusion.u_ref, bf16[3,16,16,128]{3,2,1,0:T(8,128)(2,1)S(1)} %bitcast.66, f32[128,128]{1,0:T(8,128)S(1)} %copy-done.7, f32[512,256]{1,0:T(8,128)S(1)} %copy-done.2, ...), custom_call_target="tpu_custom_call" | custom-call | tf_op jit(solution)/shard_map/project/pallas_call | solution.py:304
  189.5 0.1 convert_reduce_fusion.2
  189.6 8.0 %fusion.14 = f32[3,256]{1,0:T(4,128)S(1)} fusion(bf16[32768,256]{1,0:T(8,128)(2,1)} %fusion.3, bf16[1,3,256,128]{3,2,1,0:T(8,128)(2,1)S(1)} %bitcast.63), kind=kOutput, calls=%fused_computation.38 | convolution fusion | flops 50331648 | bytes 16976896 | tf_op jit(solution)/shard_map/dot_general | solution.py:70
  197.6 16.8 %convert_reduce_fusion = (f32[256]{0:T(256)S(1)}, bf16[32768,256]{1,0:T(8,128)(2,1)}) fusion(bf16[32768,256]{1,0:T(8,128)(2,1)} %fusion.3, bf16[3,256]{1,0:T(4,128)(2,1)S(1)} %copy-done.11, bf16[1,3,256,128]{3,2,1,0:T(8,128)(2,1)S(1)} %bitcast.64), kind=kOutput, calls=%fused_computation.13 | convolution fusion | flops 109051648 | bytes 33753600 | tf_op jit(solution)/shard_map/dot_general | solution.py:474
  214.4 14.1 %fusion.30 = f32[256,256]{1,0:T(8,128)S(1)} fusion(bf16[32768,256]{1,0:T(8,128)(2,1)} %get-tuple-element.79, bf16[32768,256]{1,0:T(8,128)(2,1)} %fusion.2), kind=kOutput, calls=%fused_computation.76 | convolution fusion | flops 4294967296 | bytes 33816576 | tf_op jit(solution)/shard_map/dot_general | solution.py:70
  228.5 20.0 %convert_reduce_fusion.1 = (f32[256]{0:T(256)S(1)}, bf16[32768,256]{1,0:T(8,128)(2,1)}) fusion(bf16[32768,256]{1,0:T(8,128)(2,1)} %fusion.2, bf16[32768,256]{1,0:T(8,128)(2,1)} %get-tuple-element.79, bf16[256,256]{1,0:T(8,128)(2,1)S(1)} %copy-done), kind=kOutput, calls=%fused_computation.14 | convolution fusion | flops 4353687552 | bytes 50463744 | tf_op jit(solution)/shard_map/dot_general | solution.py:478
  248.5 0.6 reduce_sum.107
  249.1 8.2 %fusion.31 = f32[256,12]{1,0:T(8,128)S(1)} fusion(bf16[32768,256]{1,0:T(8,128)(2,1)} %get-tuple-element.77, bf16[12,32768]{1,0:T(8,128)(2,1)S(1)} %bitcast.77), kind=kOutput, calls=%fused_computation.77 | convolution fusion | flops 201326592 | bytes 17575936 | tf_op jit(solution)/shard_map/dot_general | solution.py:70
  257.3 0.1 reshape.171
  257.4 0.1 reshape.170
  257.5 0.7 concatenate.23
  258.4 24.0 %reduce_all.1 = f32[128,5,128]{2,1,0:T(8,128)S(1)} custom-call(f32[128,5,128]{2,1,0:T(8,128)S(1)} %pad_maximum_fusion.1.part_ref), custom_call_target="tpu_custom_call" | custom-call | tf_op jit(solution)/shard_map/reduce_all/pallas_call | solution.py:393
  282.4 0.7 multiply_reduce_fusion
  283.2 0.6 multiply_reduce_fusion.1
  283.8 0.6 slice.145
  285.8 0.5 split.24
  286.3 0.6 fusion.29
  286.9 0.8 div.34
  287.7 0.6 reshape.175
  288.3 0.1 reshape.174
  288.5 0.7 copy.31
  289.8 0.7 copy.49
  290.5 0.7 copy.50
  (43 shorter events, 0.6 us)
Async XLA Ops:
  0.6 125.4 %copy-start = (bf16[256,256]{1,0:T(8,128)(2,1)S(1)}, bf16[256,256]{1,0:T(8,128)(2,1)}, u32[]{:S(2)}) copy-start(bf16[256,256]{1,0:T(8,128)(2,1)} %param.27) | copy-start | bytes 393220
  1.4 101.0 %collective-permute-start = (bf16[3,1,16,128]{3,2,1,0:T(8,128)(2,1)S(1)}, bf16[3,1,16,128]{3,2,1,0:T(8,128)(2,1)S(1)}, u32[]{:S(2)}, u32[]{:S(2)}) collective-permute-start(bf16[3,1,16,128]{3,2,1,0:T(8,128)(2,1)S(1)} %get-tuple-element.72), channel_id=1, source_target_pairs={{0,4},{4,8},{8,12},{12,16},{16,20},{20,24},{24,28},{1,5},{5,9},{9,... | collective-permute-start | bytes 36872 | tf_op jit(solution)/shard_map/ppermute | solution.py:32
  5.3 97.1 %collective-permute-start.1 = (bf16[3,1,16,128]{3,2,1,0:T(8,128)(2,1)S(1)}, bf16[3,1,16,128]{3,2,1,0:T(8,128)(2,1)S(1)}, u32[]{:S(2)}, u32[]{:S(2)}) collective-permute-start(bf16[3,1,16,128]{3,2,1,0:T(8,128)(2,1)S(1)} %get-tuple-element.73), channel_id=1, source_target_pairs={{4,0},{8,4},{12,8},{16,12},{20,16},{24,20},{28,24},{5,1},{9,5},{13... | collective-permute-start | bytes 36872 | tf_op jit(solution)/shard_map/ppermute | solution.py:35
  103.4 9.3 %collective-permute-start.2 = (bf16[3,18,1,128]{3,2,1,0:T(2,128)(2,1)S(1)}, bf16[3,18,1,128]{3,2,1,0:T(2,128)(2,1)S(1)}, u32[]{:S(2)}, u32[]{:S(2)}) collective-permute-start(bf16[3,18,1,128]{3,2,1,0:T(2,128)(2,1)S(1)} %get-tuple-element.70), channel_id=1, source_target_pairs={{0,1},{1,2},{2,3},{4,5},{5,6},{6,7},{8,9},{9,10},{10,11},{12,13},{... | collective-permute-start | bytes 41480 | tf_op jit(solution)/shard_map/ppermute | solution.py:32
  104.7 8.0 %collective-permute-start.3 = (bf16[3,18,1,128]{3,2,1,0:T(2,128)(2,1)S(1)}, bf16[3,18,1,128]{3,2,1,0:T(2,128)(2,1)S(1)}, u32[]{:S(2)}, u32[]{:S(2)}) collective-permute-start(bf16[3,18,1,128]{3,2,1,0:T(2,128)(2,1)S(1)} %get-tuple-element.71), channel_id=1, source_target_pairs={{1,0},{2,1},{3,2},{5,4},{6,5},{7,6},{9,8},{10,9},{11,10},{13,12},{... | collective-permute-start | bytes 41480 | tf_op jit(solution)/shard_map/ppermute | solution.py:35
  116.6 9.4 %copy-start.12 = (f32[256]{0:T(256)S(1)}, f32[256]{0:T(256)}, u32[]{:S(2)}) copy-start(f32[256]{0:T(256)} %param.28) | copy-start | bytes 3076
  126.0 11.5 %copy-start.10 = (f32[3]{0:T(128)S(1)}, f32[3]{0:T(128)}, u32[]{:S(2)}) copy-start(f32[3]{0:T(128)} %param.30) | copy-start | bytes 40
  126.0 11.5 %copy-start.11 = (bf16[3,256]{1,0:T(4,128)(2,1)S(1)}, bf16[3,256]{1,0:T(4,128)(2,1)}, u32[]{:S(2)}) copy-start(bf16[3,256]{1,0:T(4,128)(2,1)} %param.29) | copy-start | bytes 4612
  137.5 10.5 %copy-start.9 = (bf16[1,3,16,16,128]{4,3,2,1,0:T(8,128)(2,1)S(1)}, bf16[1,3,16,16,128]{4,3,2,1,0:T(8,128)(2,1)}, u32[]{:S(2)}) copy-start(bf16[1,3,16,16,128]{4,3,2,1,0:T(8,128)(2,1)} %param.23) | copy-start | bytes 589828
  137.5 11.2 %copy-start.1 = (f32[256,512]{1,0:T(8,128)S(1)}, f32[256,512]{1,0:T(8,128)}, u32[]{:S(2)}) copy-start(f32[256,512]{1,0:T(8,128)} %constant.101.clone.out_y) | copy-start | bytes 1572868
  137.5 11.2 %copy-start.2 = (f32[512,256]{1,0:T(8,128)S(1)}, f32[512,256]{1,0:T(8,128)}, u32[]{:S(2)}) copy-start(f32[512,256]{1,0:T(8,128)} %constant.100.clone.in_y) | copy-start | bytes 1572868
  137.5 11.2 %copy-start.3 = (bf16[1,3,16,16,128]{4,3,2,1,0:T(8,128)(2,1)S(1)}, bf16[1,3,16,16,128]{4,3,2,1,0:T(8,128)(2,1)}, u32[]{:S(2)}) copy-start(bf16[1,3,16,16,128]{4,3,2,1,0:T(8,128)(2,1)} %param.24) | copy-start | bytes 589828
  137.6 11.2 %copy-start.4 = (f32[128,256]{1,0:T(8,128)S(1)}, f32[128,256]{1,0:T(8,128)}, u32[]{:S(2)}) copy-start(f32[128,256]{1,0:T(8,128)} %constant.104.clone.plane) | copy-start | bytes 393220
  137.6 11.2 %copy-start.5 = (f32[128,192]{1,0:T(8,128)S(1)}, f32[128,192]{1,0:T(8,128)}, u32[]{:S(2)}) copy-start(f32[128,192]{1,0:T(8,128)} %constant.102.clone.in_x) | copy-start | bytes 294916
  137.6 11.2 %copy-start.6 = (f32[192,128]{1,0:T(8,128)S(1)}, f32[192,128]{1,0:T(8,128)}, u32[]{:S(2)}) copy-start(f32[192,128]{1,0:T(8,128)} %constant.103.clone.out_x) | copy-start | bytes 294916
  137.6 11.2 %copy-start.7 = (f32[128,128]{1,0:T(8,128)S(1)}, f32[128,128]{1,0:T(8,128)}, u32[]{:S(2)}) copy-start(f32[128,128]{1,0:T(8,128)} %constant.99.clone.base_z) | copy-start | bytes 196612
  137.6 11.2 %copy-start.8 = (f32[32,1,256]{2,1,0:T(1,128)S(1)}, f32[32,1,256]{2,1,0:T(1,128)}, u32[]{:S(2)}) copy-start(f32[32,1,256]{2,1,0:T(1,128)} %constant.105.clone.level) | copy-start | bytes 98308

commit v2 on v1

v2 whole, which is shorter than its diff:
```python
import functools
import math

import jax
import jax.numpy as jnp
import numpy as np
from jax import lax
from jax.experimental import pallas as pl
from jax.experimental.pallas import tpu as pltpu
from jax.sharding import PartitionSpec as P

ITERS = 20
MESH = pl.DeviceIdType.MESH
HIGHEST = lax.Precision.HIGHEST
F32 = jnp.float32
BF16 = jnp.bfloat16

inflow = 1.0
step_dt = 0.4
viscosity = 0.1
epsilon_rms = 1e-06

ROWS = 24
LIVE = 18
SLOTS = 32
FIRST = 8
STEP = 2
CHANNELS = 16
FEATS = 12


def sines(count):
    index = np.arange(1, count + 1, dtype=np.float64)
    return math.sqrt(2.0 / (count + 1)) * np.sin(math.pi * np.outer(index, index) / (count + 1))


def cosines(count):
    return 2.0 * np.cos(math.pi * np.arange(1, count + 1, dtype=np.float64) / (count + 1))


def solve_tables(n_gx, n_gy, span_x, span_y, depth):
    nx, ny = n_gx * span_x, n_gy * span_y
    group = n_gx * n_gy
    modes = depth // group
    base_x, base_y = sines(nx), sines(ny)
    in_y = np.zeros((n_gy, modes, SLOTS, modes, ny))
    for gy in range(n_gy):
        for slot in range(FIRST - 1, FIRST + span_y + 1):
            y = gy * span_y + slot - FIRST
            if 0 <= y < ny:
                for mode in range(modes):
                    in_y[gy, mode, slot, mode] = base_y[y]
    in_y = in_y.reshape(n_gy * modes * SLOTS, modes * ny)
    in_x = np.zeros((nx, n_gx, ROWS))
    for gx in range(n_gx):
        for row in range(LIVE):
            x = gx * span_x + (row if row < span_x else (-1 if row == span_x else span_x))
            if 0 <= x < nx:
                in_x[:, gx, row] = base_x[x]
    in_x = in_x.reshape(nx, n_gx * ROWS)
    plane = np.tile((cosines(nx)[:, None] + cosines(ny)[None, :]) / 6.0, (1, modes))
    level = np.repeat((cosines(depth) / 6.0).reshape(modes, group).T, ny, axis=1)
    tables = (sines(depth), in_y, in_y.T, in_x, in_x.T, plane, level[:, None, :])
    return tuple(np.ascontiguousarray(table, dtype=np.float32) for table in tables)


def dot_full(left, right):
    return jnp.dot(left, right, precision=HIGHEST, preferred_element_type=jnp.float32)


def depth_difference(values):
    dim = values.ndim - 1
    depth = values.shape[dim]
    lane = lax.broadcasted_iota(jnp.int32, values.shape, dim)
    above = jnp.where(lane == depth - 1, 0.0, pltpu.roll(values, depth - 1, dim))
    below = jnp.where(lane == 0, 0.0, pltpu.roll(values, 1, dim))
    return above - below


def swap_groups(pieces, stride):
    count = len(pieces)
    lane = lax.broadcasted_iota(jnp.int32, pieces[0].shape, 1) // stride
    results = []
    for b in range(count):
        result = None
        for a in range(count):
            shift = ((a - b) * stride) % (count * stride)
            moved = pieces[a] if shift == 0 else pltpu.roll(pieces[a], shift, 1)
            result = moved if result is None else jnp.where(lane == a, moved, result)
        results.append(result)
    return results


def mm(left, right):
    return jnp.dot(left, right, preferred_element_type=F32)


def mm_cells(left, right):
    return lax.dot_general(left, right, (((1,), (1,)), ((), ())), preferred_element_type=F32)


def split_three(values):
    high = values.astype(BF16)
    rest = values - high.astype(F32)
    middle = rest.astype(BF16)
    low = (rest - middle.astype(F32)).astype(BF16)
    return high, middle, low


def column(row):
    return jnp.broadcast_to(row, (128, row.shape[1])).T[:, 0:1]


def step_kernel(
    sizes,
    v_ref,
    t_ref,
    weight_in,
    bias_in,
    weight_mid,
    bias_mid,
    weight_out,
    bias_out,
    thrust_coef,
    tile_cells,
    tile_turbine,
    tile_weight,
    base_z,
    in_y,
    out_y,
    in_x,
    out_x,
    plane,
    level,
    new_ref,
    loss_ref,
    step_in,
    step_bin,
    step_mid,
    step_bmid,
    step_out,
    step_bout,
    force_ref,
    rext,
    pext,
    vpad,
    tend,
    field,
    gain,
    features,
    one,
    two,
    stage,
    forces,
    result,
    w_one,
    w_out,
    w_mid_back,
    w_out_back,
    b_mid,
    coef,
    g_mid,
    g_out,
    g_in,
    small,
    halo_send,
    halo_x,
    halo_y,
    disk_send,
    disk_recv,
    send_a,
    recv_a,
    send_b,
    recv_b,
    recv_c,
    recv_d,
    cross,
    mine,
    halo_ssem,
    halo_rsem,
    send_sem,
    recv_sem,
    cross_ssem,
    cross_rsem,
):
    n_case, n_gx, n_gy = sizes
    case, gx, gy = lax.axis_index("case"), lax.axis_index("gx"), lax.axis_index("gy")
    group = n_gx * n_gy
    me = gy * n_gx + gx
    span_x, span_y, depth = v_ref.shape[2:]
    modes = depth // group
    units = weight_mid.shape[0]
    last = FIRST + span_y
    steps = span_x // STEP
    lines = STEP * span_y

    def device(index):
        return (case, lax.rem(index, n_gx), index // n_gx)

    for side in range(2):
        recv_a[side, :, span_x:, :] = jnp.zeros((group, ROWS - span_x, depth), F32)

    barrier = pltpu.get_barrier_semaphore()

    def greet(step, carry):
        pl.semaphore_signal(
            barrier,
            inc=1,
            device_id=device(lax.rem(me + step, group)),
            device_id_type=MESH,
        )
        return carry

    lax.fori_loop(1, group, greet, 0)
    for step in range(1, n_case):
        pl.semaphore_signal(
            barrier,
            inc=1,
            device_id=(lax.rem(case + step, n_case), gx, gy),
            device_id_type=MESH,
        )

    row_z = lax.broadcasted_iota(jnp.int32, (depth, 128), 0)
    row_xy = lax.broadcasted_iota(jnp.int32, (span_x * span_y, 128), 0)
    lane = lax.broadcasted_iota(jnp.int32, (1, 128), 1)
    tiles = tile_cells.shape[0]
    stream = v_ref[0, 0].reshape(span_x * span_y, depth)
    disk_sum = jnp.zeros((1, 128), F32)
    disk_area = jnp.zeros((1, 128), F32)
    for tile in range(tiles):
        cells = tile_cells[tile : tile + 1, :]
        weights = tile_weight[tile : tile + 1, :]
        pick_z = jnp.where(row_z == cells % depth, 1.0, 0.0).astype(BF16)
        levels = mm(stream, pick_z)
        sampled = jnp.sum(jnp.where(row_xy == cells // depth, levels, 0.0), 0, keepdims=True)
        weighted = jnp.sum(weights * (sampled + inflow), 1, keepdims=True)
        area = jnp.sum(weights, 1, keepdims=True)
        match = lane == tile_turbine[tile]
        disk_sum = disk_sum + jnp.where(match, weighted, 0.0)
        disk_area = disk_area + jnp.where(match, area, 0.0)
    disk_send[0:1, :] = disk_sum
    disk_send[1:2, :] = disk_area

    vpad[...] = jnp.zeros_like(vpad)
    for component in range(3):
        values = v_ref[0, component].astype(F32)
        vpad[component, 1 : span_x + 1, FIRST:last, :] = values
        halo_send[0, component] = values[:, 0, :].astype(BF16)
        halo_send[1, component] = values[:, span_y - 1, :].astype(BF16)

    w_one[...] = jnp.zeros_like(w_one)
    w_one[:, 0:FEATS] = weight_in[...].astype(F32)
    for place, part in enumerate(split_three(column(bias_in[...]))):
        w_one[:, FEATS + place : FEATS + place + 1] = part.astype(F32)
    w_out[...] = jnp.zeros_like(w_out)
    w_out[0:3, :] = weight_out[...].astype(F32)
    w_out_back[...] = w_out[...].T.astype(BF16)
    w_mid_back[...] = weight_mid[...].astype(F32).T.astype(BF16)
    b_mid[...] = column(bias_mid[...])
    coef[...] = jnp.zeros_like(coef)
    coef[0:1, 0 : thrust_coef.shape[1]] = thrust_coef[...]
    line_row = lax.broadcasted_iota(jnp.int32, stage.shape, 1)
    stage[...] = jnp.where((line_row >= FEATS) & (line_row < FEATS + 3), 1.0, 0.0)
    forces[...] = jnp.where(line_row == 3, 1.0, 0.0)

    ratio = plane[...] + level[me]
    total = jnp.ones_like(ratio)
    for _ in range(ITERS - 1):
        total = total * ratio + 1.0
    gain[...] = total * (-1.0 / 24.0)
    rext[...] = jnp.zeros_like(rext)

    pl.semaphore_wait(barrier, group - 1 + n_case - 1)

    copies = []
    for side, (source, place) in enumerate(((span_x - 1, 1), (0, n_gx - 1))):
        copies.append(
            pltpu.make_async_remote_copy(
                src_ref=v_ref.at[0, :, source],
                dst_ref=halo_x.at[side],
                send_sem=halo_ssem.at[side],
                recv_sem=halo_rsem.at[side],
                device_id=(case, lax.rem(gx + place, n_gx), gy),
                device_id_type=MESH,
            )
        )
    for side, (source, place) in enumerate(((1, 1), (0, n_gy - 1))):
        copies.append(
            pltpu.make_async_remote_copy(
                src_ref=halo_send.at[source],
                dst_ref=halo_y.at[side],
                send_sem=halo_ssem.at[2 + side],
                recv_sem=halo_rsem.at[2 + side],
                device_id=(case, gx, lax.rem(gy + place, n_gy)),
                device_id_type=MESH,
            )
        )
    for copy in copies:
        copy.start()

    def send_disk(step, carry):
        peer = lax.rem(me + step, group)
        pltpu.make_async_remote_copy(
            src_ref=disk_send,
            dst_ref=disk_recv.at[me],
            send_sem=send_sem.at[6],
            recv_sem=recv_sem.at[6],
            device_id=device(peer),
            device_id_type=MESH,
        ).start()
        return carry

    lax.fori_loop(1, group, send_disk, 0)
    disk_recv[me] = disk_send[...]

    for copy in copies:
        copy.wait()
    for component in range(3):
        for side, (row, inside) in enumerate(((0, gx > 0), (span_x + 1, gx < n_gx - 1))):
            values = halo_x[side, component].astype(F32)
            vpad[component, row, FIRST:last, :] = jnp.where(inside, values, 0.0)
        for side, (slot, inside) in enumerate(((FIRST - 1, gy > 0), (last, gy < n_gy - 1))):
            values = halo_y[side, component].astype(F32)
            vpad[component, 1 : span_x + 1, slot, :] = jnp.where(inside, values, 0.0)

    def forward(step, carry):
        base = step * STEP
        rows = pl.ds(base + 1, STEP)
        tendency = []
        speeds = []
        slopes = []
        for component in range(3):
            middle = vpad[component, rows, FIRST:last, :]
            above_x = vpad[component, pl.ds(base + 2, STEP), FIRST:last, :]
            below_x = vpad[component, pl.ds(base, STEP), FIRST:last, :]
            above_y = vpad[component, rows, FIRST + 1 : last + 1, :]
            below_y = vpad[component, rows, FIRST - 1 : last - 1, :]
            level_of = lax.broadcasted_iota(jnp.int32, middle.shape, 2)
            above_z = jnp.where(level_of == depth - 1, 0.0, pltpu.roll(middle, depth - 1, 2))
            below_z = jnp.where(level_of == 0, 0.0, pltpu.roll(middle, 1, 2))
            slopes.append(
                [
                    0.5 * (above_x - below_x),
                    0.5 * (above_y - below_y),
                    0.5 * (above_z - below_z),
                ]
            )
            around = above_x + below_x + above_y + below_y + above_z + below_z
            tendency.append(viscosity * (around - 6.0 * middle))
            speeds.append(middle)
        for component in range(3):
            for axis in range(3):
                stage[:, axis * 3 + component, :] = slopes[component][axis].reshape(lines, depth)
            stage[:, 9 + component, :] = speeds[component].reshape(lines, depth)
            advect = (
                (speeds[0] + inflow) * slopes[component][0]
                + speeds[1] * slopes[component][1]
                + speeds[2] * slopes[component][2]
            )
            tendency[component] = tendency[component] - advect
        for line in range(lines):
            features[step, :, line * depth : (line + 1) * depth] = stage[line].astype(BF16)
        inputs = features[step]
        hidden_one = jnp.tanh(mm(w_one[...].astype(BF16), inputs)).astype(BF16)
        one[step] = hidden_one
        hidden_two = jnp.tanh(mm(weight_mid[...], hidden_one) + b_mid[...]).astype(BF16)
        two[step] = hidden_two
        closure = mm(w_out[...].astype(BF16), hidden_two)
        for line in range(lines):
            result[line] = closure[0:8, line * depth : (line + 1) * depth]
        for component in range(3):
            added = result[:, component, :].reshape(STEP, span_y, depth) + bias_out[component]
            tend[component, pl.ds(base, STEP)] = tendency[component] + added
        return carry

    lax.fori_loop(0, steps, forward, 0)

    landed = disk_recv.at[pl.ds(0, group - 1)]
    pltpu.make_async_copy(landed, landed, recv_sem.at[6]).wait()
    pltpu.make_async_copy(landed, landed, send_sem.at[6]).wait()
    disks = jnp.sum(disk_recv[...], 0)
    disk_speed = disks[0:1, :] / jnp.maximum(disks[1:2, :], 1.0)
    thrust = -0.5 * coef[0:1, :] * disk_speed * jnp.abs(disk_speed)
    pushed = jnp.zeros((span_x * span_y, depth), F32)
    for tile in range(tiles):
        cells = tile_cells[tile : tile + 1, :]
        row_thrust = jnp.sum(
            jnp.where(lane == tile_turbine[tile], thrust, 0.0), 1, keepdims=True
        )
        spread = tile_weight[tile : tile + 1, :] * row_thrust
        pick_xy = jnp.where(row_xy == cells // depth, 1.0, 0.0).astype(BF16)
        placed = jnp.where(row_z == cells % depth, spread, 0.0)
        for part in split_three(placed):
            pushed = pushed + mm_cells(pick_xy, part)
    tend[0] = tend[0] + pushed.reshape(span_x, span_y, depth)
    for component in range(3):
        speed = vpad[component, 1 : span_x + 1, FIRST:last, :]
        provisional = (speed + step_dt * tend[component]).astype(BF16)
        tend[component] = provisional.astype(F32)

    def exchange(number, outgoing, incoming, same=False):
        def start(step, carry):
            peer = lax.rem(me + step, group)
            source = outgoing if same else outgoing.at[peer]
            pltpu.make_async_remote_copy(
                src_ref=source.at[pl.ds(0, LIVE)],
                dst_ref=incoming.at[me, pl.ds(0, LIVE)],
                send_sem=send_sem.at[number],
                recv_sem=recv_sem.at[number],
                device_id=device(peer),
                device_id_type=MESH,
            ).start()
            return carry

        lax.fori_loop(1, group, start, 0)
        if same:
            incoming[me, pl.ds(0, LIVE)] = outgoing[pl.ds(0, LIVE)]
        else:
            incoming[me, pl.ds(0, LIVE)] = outgoing[me, pl.ds(0, LIVE)]
        landed = incoming.at[pl.ds(0, group - 1), pl.ds(0, LIVE)]
        pltpu.make_async_copy(landed, landed, recv_sem.at[number]).wait()

    def sent(number):
        left = send_a.at[pl.ds(0, group - 1), pl.ds(0, LIVE)]
        pltpu.make_async_copy(left, left, send_sem.at[number]).wait()

    def solve(number, q_x, q_y, q_z):
        zero_x = jnp.zeros((1, span_y, depth), F32)
        inner = jnp.concatenate([q_x[1:], zero_x], 0) - jnp.concatenate([zero_x, q_x[:-1]], 0)
        inner = inner + depth_difference(q_z)
        wide = jnp.concatenate(
            [
                jnp.zeros((span_x, FIRST, depth), F32),
                q_y,
                jnp.zeros((span_x, SLOTS - last, depth), F32),
            ],
            1,
        )
        rext[0:span_x] = pltpu.roll(wide, SLOTS - 1, 1) - pltpu.roll(wide, 1, 1)
        rext[0:span_x, FIRST:last, :] = rext[0:span_x, FIRST:last, :] + inner
        rext[span_x, FIRST:last, :] = q_x[0]
        rext[span_x + 1, FIRST:last, :] = -q_x[span_x - 1]
        if number > 0:
            sent(2 * number - 2)
        for part in range(rext.shape[0] // modes):
            cells = rext[part * modes : (part + 1) * modes].reshape(modes * SLOTS, depth)
            turned = dot_full(cells, base_z[...]).T
            pieces = [turned[m * group : (m + 1) * group] for m in range(modes)]
            for inside, piece in enumerate(swap_groups(pieces, SLOTS)):
                if part * modes + inside < LIVE:
                    send_a[:, part * modes + inside, :] = piece
        arrived = recv_a.at[number]
        exchange(2 * number, send_a, arrived)
        along_y = None
        for block in range(n_gy):
            rows = arrived[block * n_gx : (block + 1) * n_gx].reshape(n_gx * ROWS, depth)
            part = dot_full(rows, in_y[block * depth : (block + 1) * depth, :])
            along_y = part if along_y is None else along_y + part
        spectrum = dot_full(in_x[...], along_y) * gain[...]
        back = dot_full(out_x[...], spectrum)
        if number > 0:
            sent(2 * number - 1)
        for block in range(n_gy):
            part = dot_full(back, out_y[:, block * depth : (block + 1) * depth])
            send_b[block * n_gx : (block + 1) * n_gx] = part.reshape(n_gx, ROWS, depth)
        arrived = recv_b.at[number]
        exchange(2 * number + 1, send_b, arrived)
        for part in range(pext.shape[0] // modes):
            pieces = [
                arrived[:, min(part * modes + inside, LIVE - 1), :] for inside in range(modes)
            ]
            turned = jnp.concatenate(swap_groups(pieces, SLOTS), 0).T
            pext[part * modes : (part + 1) * modes] = dot_full(turned, base_z[...]).reshape(
                modes, SLOTS, depth
            )

    def slope():
        middle = pext[0:span_x, FIRST:last, :]
        low = pext[span_x : span_x + 1, FIRST:last, :]
        high = pext[span_x + 1 : span_x + 2, FIRST:last, :]
        along_x = jnp.concatenate([middle[1:], high], 0) - jnp.concatenate([low, middle[:-1]], 0)
        along_y = (
            pext[0:span_x, FIRST + 1 : last + 1, :] - pext[0:span_x, FIRST - 1 : last - 1, :]
        )
        return along_x, along_y, depth_difference(middle)

    solve(0, tend[0], tend[1], tend[2])
    cost = jnp.zeros((1, depth), F32)
    for component, change in enumerate(slope()):
        updated = tend[component] - change
        new_ref[0, component] = updated.astype(BF16)
        mismatch = updated - t_ref[0, component].astype(F32)
        cost = cost + jnp.sum(
            (mismatch * mismatch).reshape(span_x * span_y, depth), 0, keepdims=True
        )
        field[component] = 2.0 * mismatch
    small[...] = jnp.zeros_like(small)
    small[43:44, :] = cost
    solve(1, field[0], field[1], field[2])
    for component, change in enumerate(slope()):
        force = (step_dt * (field[component] - change)).astype(BF16)
        force_ref[0, component] = force
        force = force.astype(F32)
        field[component] = force
        small[40 + component : 41 + component, :] = jnp.sum(
            force.reshape(span_x * span_y, depth), 0, keepdims=True
        )

    g_mid[...] = jnp.zeros_like(g_mid)
    g_out[...] = jnp.zeros_like(g_out)
    g_in[...] = jnp.zeros_like(g_in)

    def backward(step, carry):
        base = step * STEP
        for component in range(3):
            forces[:, component, :] = field[component, pl.ds(base, STEP)].reshape(lines, depth)
        force = jnp.concatenate([forces[line].astype(BF16) for line in range(lines)], 1)
        hidden_two = two[step]
        hidden_one = one[step]
        value = hidden_two.astype(F32)
        delta_two = (mm(w_out_back[...], force) * (1.0 - value * value)).astype(BF16)
        g_out[...] = g_out[...] + mm_cells(force, hidden_two)
        g_mid[0:units, :] = g_mid[0:units, :] + mm_cells(hidden_one, delta_two)
        g_mid[units:, :] = g_mid[units:, :] + mm_cells(force, delta_two)
        value = hidden_one.astype(F32)
        delta_one = (mm(w_mid_back[...], delta_two) * (1.0 - value * value)).astype(BF16)
        g_in[...] = g_in[...] + mm_cells(features[step], delta_one)
        return carry

    lax.fori_loop(0, steps, backward, 0)

    sent(2)
    for half in range(2):
        lanes = slice(half * 128, half * 128 + 128)
        small[half * CHANNELS : (half + 1) * CHANNELS, :] = g_in[:, lanes]
        small[32 + half : 33 + half, :] = g_mid[units + 3 : units + 4, lanes]
        small[34 + 3 * half : 37 + 3 * half, :] = g_out[0:3, lanes]
    middle = g_mid[0:units, :].T
    for owner in range(group):
        tile = middle[owner * 8 : (owner + 1) * 8, :]
        send_a[owner, 0:8, :] = tile[:, 0:128]
        send_a[owner, 8:16, :] = tile[:, 128:256]
        send_a[owner, 16:18, :] = small[2 * owner : 2 * owner + 2, :]
    exchange(4, send_a, recv_c)
    mine[...] = jnp.sum(recv_c[:, 0:LIVE, :], 0)
    copies = []
    for step in range(1, n_case):
        copies.append(
            pltpu.make_async_remote_copy(
                src_ref=mine,
                dst_ref=cross.at[step - 1],
                send_sem=cross_ssem.at[step - 1],
                recv_sem=cross_rsem.at[step - 1],
                device_id=(lax.rem(case + step, n_case), gx, gy),
                device_id_type=MESH,
            )
        )
    for copy in copies:
        copy.start()
    for copy in copies:
        copy.wait()
    places = []
    for source in range(n_case):
        step = lax.rem(case - source + n_case, n_case)
        there = cross[lax.max(step - 1, 0)]
        places.append(jnp.where(step == 0, mine[...], there))
    whole = places[0]
    for place in places[1:]:
        whole = whole + place
    sent(3)
    send_b[0, 0:LIVE, :] = whole
    exchange(5, send_b.at[0], recv_d, True)
    for owner in range(group):
        small[2 * owner : 2 * owner + 2, :] = recv_d[owner, 16:18, :]
    big = recv_d[:, 0:16, :].reshape(group * 16, 128)
    rest = small[...]
    bout = jnp.sum(rest[40:43], 1, keepdims=True)
    cost = jnp.sum(rest[43:44], 1, keepdims=True)
    row = lax.broadcasted_iota(jnp.int32, rest.shape, 0)
    inner_row = row % CHANNELS
    counted = ((row < 32) & (inner_row <= FEATS)) | ((row >= 32) & (row < 40))
    kept = jnp.where(counted, rest, 0.0)
    squares = jnp.sum(jnp.sum(big * big, 0, keepdims=True), 1, keepdims=True)
    squares = squares + jnp.sum(jnp.sum(kept * kept, 0, keepdims=True), 1, keepdims=True)
    squares = squares + jnp.sum(bout * bout, 0, keepdims=True)
    entries = units * FEATS + units + units * units + units + 3 * units + 3
    scale_rms = jnp.sqrt(squares / entries + epsilon_rms)
    for owner in range(group):
        step_mid[owner * 8 : (owner + 1) * 8, 0:128] = recv_d[owner, 0:8, :] / scale_rms
        step_mid[owner * 8 : (owner + 1) * 8, 128:256] = recv_d[owner, 8:16, :] / scale_rms
    scaled = rest / scale_rms
    for half in range(2):
        lanes = slice(half * 128, half * 128 + 128)
        block = scaled[half * CHANNELS : (half + 1) * CHANNELS, :]
        tall = jnp.concatenate([block, jnp.zeros((128 - CHANNELS, 128), F32)], 0).T
        step_in[lanes, :] = tall[:, 0:FEATS]
        step_bin[0:1, lanes] = block[FEATS : FEATS + 1, :]
        step_bmid[0:1, lanes] = scaled[32 + half : 33 + half, :]
        step_out[:, lanes] = scaled[34 + 3 * half : 37 + 3 * half, :]
    step_bout[...] = bout / scale_rms
    cells_all = 3 * n_case * group * span_x * span_y * depth
    loss_ref[...] = cost / cells_all
    sent(4)
    sent(5)


def on_device(
    velocity,
    target,
    weight_in,
    bias_in,
    weight_mid,
    bias_mid,
    weight_out,
    bias_out,
    thrust_coef,
    tile_cells,
    tile_turbine,
    tile_weight,
):
    sizes = tuple(lax.axis_size(axis) for axis in ("case", "gx", "gy"))
    n_case, n_gx, n_gy = sizes
    group = n_gx * n_gy
    _, _, span_x, span_y, depth = velocity.shape
    units = weight_mid.shape[0]
    tables = solve_tables(n_gx, n_gy, span_x, span_y, depth)
    vmem = pl.BlockSpec(memory_space=pltpu.VMEM)
    smem = pl.BlockSpec(memory_space=pltpu.SMEM)
    steps = span_x // STEP
    lines = STEP * span_y
    wide = lines * depth
    outs = pl.pallas_call(
        functools.partial(step_kernel, sizes),
        out_shape=(
            jax.ShapeDtypeStruct(velocity.shape, BF16),
            jax.ShapeDtypeStruct((1, 1), F32),
            jax.ShapeDtypeStruct((units, FEATS), F32),
            jax.ShapeDtypeStruct((1, units), F32),
            jax.ShapeDtypeStruct((units, units), F32),
            jax.ShapeDtypeStruct((1, units), F32),
            jax.ShapeDtypeStruct((3, units), F32),
            jax.ShapeDtypeStruct((3, 1), F32),
            jax.ShapeDtypeStruct(velocity.shape, BF16),
        ),
        in_specs=[vmem] * 7 + [smem, vmem, vmem, smem, vmem] + [vmem] * len(tables),
        out_specs=(vmem,) * 9,
        scratch_shapes=[
            pltpu.VMEM((span_x + 4, SLOTS, depth), F32),
            pltpu.VMEM((span_x + 4, SLOTS, depth), F32),
            pltpu.VMEM((3, span_x + 2, SLOTS, depth), F32),
            pltpu.VMEM((3, span_x, span_y, depth), F32),
            pltpu.VMEM((3, span_x, span_y, depth), F32),
            pltpu.VMEM(tables[5].shape, F32),
            pltpu.VMEM((steps, CHANNELS, wide), BF16),
            pltpu.VMEM((steps, units, wide), BF16),
            pltpu.VMEM((steps, units, wide), BF16),
            pltpu.VMEM((lines, CHANNELS, depth), F32),
            pltpu.VMEM((lines, CHANNELS, depth), F32),
            pltpu.VMEM((lines, 8, depth), F32),
            pltpu.VMEM((units, CHANNELS), F32),
            pltpu.VMEM((CHANNELS, units), F32),
            pltpu.VMEM((units, units), BF16),
            pltpu.VMEM((units, CHANNELS), BF16),
            pltpu.VMEM((units, 1), F32),
            pltpu.VMEM((8, 128), F32),
            pltpu.VMEM((units + CHANNELS, units), F32),
            pltpu.VMEM((CHANNELS, units), F32),
            pltpu.VMEM((CHANNELS, units), F32),
            pltpu.VMEM((2 * group, 128), F32),
            pltpu.VMEM((2, 3, span_x, depth), BF16),
            pltpu.VMEM((2, 3, span_y, depth), BF16),
            pltpu.VMEM((2, 3, span_x, depth), BF16),
            pltpu.VMEM((2, 128), F32),
            pltpu.VMEM((group, 2, 128), F32),
            pltpu.VMEM((group, ROWS, depth), F32),
            pltpu.VMEM((2, group, ROWS, depth), F32),
            pltpu.VMEM((group, ROWS, depth), F32),
            pltpu.VMEM((2, group, ROWS, depth), F32),
            pltpu.VMEM((group, ROWS, depth), F32),
            pltpu.VMEM((group, ROWS, depth), F32),
            pltpu.VMEM((n_case - 1, LIVE, 128), F32),
            pltpu.VMEM((LIVE, 128), F32),
            pltpu.SemaphoreType.DMA((4,)),
            pltpu.SemaphoreType.DMA((4,)),
            pltpu.SemaphoreType.DMA((7,)),
            pltpu.SemaphoreType.DMA((7,)),
            pltpu.SemaphoreType.DMA((n_case - 1,)),
            pltpu.SemaphoreType.DMA((n_case - 1,)),
        ],
        compiler_params=pltpu.CompilerParams(
            collective_id=0, has_side_effects=True, vmem_limit_bytes=60 * 1024 * 1024
        ),
        name="flow_step",
    )(
        velocity,
        target,
        weight_in,
        bias_in[None, :],
        weight_mid,
        bias_mid[None, :],
        weight_out,
        bias_out,
        thrust_coef[None, :],
        tile_cells,
        tile_turbine,
        tile_weight,
        *tables,
    )
    new, loss, step_in, step_bin, step_mid, step_bmid, step_out, step_bout, force = outs
    return (
        new,
        loss[0, 0],
        step_in,
        step_bin[0],
        step_mid,
        step_bmid[0],
        step_out,
        step_bout[:, 0],
        force,
    )


def solution(mesh):
    placed = (
        P("case", None, "gx", "gy", None),
        P("case", None, "gx", "gy", None),
        P(),
        P(),
        P(),
        P(),
        P(),
        P(),
        P(),
        P(("gx", "gy"), None),
        P(("gx", "gy")),
        P(("gx", "gy"), None),
    )
    return jax.shard_map(
        on_device,
        mesh=mesh,
        in_specs=placed,
        out_specs=(
            P("case", None, "gx", "gy", None),
            P(),
            P(),
            P(),
            P(),
            P(),
            P(),
            P(),
            P("case", None, "gx", "gy", None),
        ),
        check_vma=False,
    )
```

time: 294 us -> 123 us (0.42)
  matrix products: 98.2 us -> 0 us
  blocking collectives: 84.1 us -> 0 us
  Pallas kernels: 64.7 us -> 111 us
  other arithmetic: 19.2 us -> 0.63 us
  starting transfers between devices: 7.77 us -> 0 us
  local copies, waits for them, and re-layouts: 14.2 us -> 8.49 us
    dot_general x8 -> x0, matrix products: 98.2 us -> none  [the longest x3 30.2 us: contract_cells(): lax.dot_general(former, latter, (((1,), (1,)), ((), ())), preferred_eleme...]
    psum x1 -> x0, blocking collectives: 84.1 us -> none  [on_device(): disk_sum, disk_area = lax.psum((disk_sum, disk_area), ('gx', 'gy'))]
    pallas_call x2 -> x1, Pallas kernels: 64.7 us -> 111 us  [on_device(): pl.pallas_call(functools.partial(step_kernel, sizes), out_shape=(jax.Shap...]
    ppermute x4 -> x0, starting transfers between devices: 7.77 us -> none  [the longest x2 5.18 us: extended_2(): lax.ppermute(lax.slice_in_dim(block, block.shape[dim] - width, None, axis...]
    gather x1 -> x0, local copies, waits for them, and re-layouts: 6.15 us -> none  [on_device(): sampled = stream_flat[tile_cells]]
    scatter-add x2 -> x0, other arithmetic: 5.99 us -> none  [the longest x1 5.96 us: on_device(): jnp.zeros((cells_dev,), jnp.float32).at[tile_cells.reshape(-1)].add(spread)]
    unnamed x32 -> x20, local copies, waits for them, and re-layouts: 2.96 us -> 8.49 us
    reduce_sum x7 -> x0, other arithmetic: 4.49 us -> none  [the longest x2 1.34 us: on_device(): squares = jnp.sum(big * big) + jnp.sum(small * small)]
  transfers between devices with their start and end apart: 4 -> 0, of which waited for: 0 -> 0; matrix products, arithmetic and copies ran while one was open for 6% -> 0% of each run, Pallas kernels for 0% -> 0%
where the time goes in v2:
time: 123 us; the launch traced here: 122 us
  Pallas kernels  111 us (90%)
  local copies, waits for them, and re-layouts  8.49 us (7%)
  between operations  2.49 us (2%)
    pallas_call x1, Pallas kernels, on_device(): pl.pallas_call(functools.partial(step_kernel, sizes), out_shape=(jax.Shap...  111 us
    unnamed x20, local copies, waits for them, and re-layouts  8.49 us

profile of v2, /device:TPU:0, one launch (start us, length us, event | category | flops | bytes accessed | tf_op | source)
XLA Modules:
  0.0 122.3 jit_solution(12227477632955986290)
XLA Ops:
  0.6 1.4 %copy.30.weight_in = bf16[256,12]{1,0:T(8,128)(2,1)} copy(bf16[256,12]{0,1:T(8,128)(2,1)} %param.21) | data formatting | bytes 12288 | tf_op args[2]
  2.1 110.7 %flow_step.1 = (bf16[1,3,16,16,128]{4,3,2,1,0:T(8,128)(2,1)}, f32[1,1]{1,0:T(1,128)}, f32[256,12]{1,0:T(8,128)}, f32[1,256]{1,0:T(1,128)}, f32[256,256]{1,0:T(8,...) custom-call(bf16[1,3,16,16,128]{4,3,2,1,0:T(8,128)(2,1)} %v_ref.1, ...), custom_call_target="tpu_custom_call" | custom-call | tf_op jit(solution)/shard_map/flow_step/pallas_call | solution.py:632
  112.8 0.0 copy-start.3
  112.8 0.7 copy-done.3
  113.5 0.6 reduce
  114.1 0.0 copy-start
  114.1 1.6 %copy.31 = f32[256,12]{0,1:T(8,128)} copy(f32[256,12]{1,0:T(8,128)} %get-tuple-element.38) | data formatting | bytes 24576
  115.8 1.6 %copy.39 = bf16[1,3,16,16,128]{4,3,2,1,0:T(8,128)(2,1)} copy(bf16[1,3,16,16,128]{4,3,2,1,0:T(8,128)(2,1)} %get-tuple-element.54) | data formatting | bytes 393216
  117.4 0.0 copy-start.5
  118.1 0.0 copy-done.5
  118.1 0.6 copy.41
  118.7 0.0 copy-done
  118.7 0.0 copy-start.4
  118.7 0.0 copy-start.2
  118.7 0.0 copy-start.1
  118.7 0.7 copy.42
  119.4 0.0 copy-done.4
  119.4 0.6 copy.43
  119.9 0.0 copy-done.2
  119.9 0.6 copy.44
  120.5 0.0 copy-done.1
  120.5 0.7 copy.45
Async XLA Ops:
  112.8 0.7 copy-start.3
  114.1 4.5 %copy-start = (f32[256,256]{1,0:T(8,128)S(1)}, f32[256,256]{1,0:T(8,128)}, u32[]{:S(2)}) copy-start(f32[256,256]{1,0:T(8,128)} %get-tuple-element.58) | copy-start | bytes 786436
  117.4 0.7 copy-start.5
  118.7 0.7 copy-start.4
  118.7 1.3 %copy-start.2 = (f32[3,256]{1,0:T(4,128)S(1)}, f32[3,256]{1,0:T(4,128)}, u32[]{:S(2)}) copy-start(f32[3,256]{1,0:T(4,128)} %get-tuple-element.60) | copy-start | bytes 9220
  118.7 1.9 %copy-start.1 = (bf16[1,3,16,16,128]{4,3,2,1,0:T(8,128)(2,1)S(1)}, bf16[1,3,16,16,128]{4,3,2,1,0:T(8,128)(2,1)}, u32[]{:S(2)}) copy-start(bf16[1,3,16,16,128]{4,3,2,1,0:T(8,128)(2,1)} %get-tuple-element.62) | copy-start | bytes 589828

commit v3 on v2

--- a/solution.py
+++ b/solution.py
@@ -11,7 +11,6 @@
 
 ITERS = 20
 MESH = pl.DeviceIdType.MESH
-HIGHEST = lax.Precision.HIGHEST
 F32 = jnp.float32
 BF16 = jnp.bfloat16
 
@@ -64,8 +63,18 @@
     return tuple(np.ascontiguousarray(table, dtype=np.float32) for table in tables)
 
 
+def split_two(values):
+    high = values.astype(BF16)
+    return high, (values - high.astype(F32)).astype(BF16)
+
+
 def dot_full(left, right):
-    return jnp.dot(left, right, precision=HIGHEST, preferred_element_type=jnp.float32)
+    left_high, left_low = split_two(left)
+    right_high, right_low = split_two(right)
+    return (
+        jnp.dot(left_low, right_high, preferred_element_type=F32)
+        + jnp.dot(left_high, right_low, preferred_element_type=F32)
+    ) + jnp.dot(left_high, right_high, preferred_element_type=F32)
 
 
 def depth_difference(values):
@@ -162,6 +171,8 @@
     g_mid,
     g_out,
     g_in,
+    g_bias,
+    columns,
     small,
     halo_send,
     halo_x,
@@ -248,10 +259,11 @@
         halo_send[0, component] = values[:, 0, :].astype(BF16)
         halo_send[1, component] = values[:, span_y - 1, :].astype(BF16)
 
-    w_one[...] = jnp.zeros_like(w_one)
-    w_one[:, 0:FEATS] = weight_in[...].astype(F32)
-    for place, part in enumerate(split_three(column(bias_in[...]))):
-        w_one[:, FEATS + place : FEATS + place + 1] = part.astype(F32)
+    stack = [weight_in[...].astype(F32)] + [
+        part.astype(F32) for part in split_three(bias_in[...])
+    ]
+    stack.append(jnp.zeros((CHANNELS - FEATS - 3, units), F32))
+    w_one[...] = jnp.concatenate(stack, 0).T.astype(BF16)
     w_out[...] = jnp.zeros_like(w_out)
     w_out[0:3, :] = weight_out[...].astype(F32)
     w_out_back[...] = w_out[...].T.astype(BF16)
@@ -261,7 +273,7 @@
     coef[0:1, 0 : thrust_coef.shape[1]] = thrust_coef[...]
     line_row = lax.broadcasted_iota(jnp.int32, stage.shape, 1)
     stage[...] = jnp.where((line_row >= FEATS) & (line_row < FEATS + 3), 1.0, 0.0)
-    forces[...] = jnp.where(line_row == 3, 1.0, 0.0)
+    forces[...] = jnp.zeros_like(forces)
 
     ratio = plane[...] + level[me]
     total = jnp.ones_like(ratio)
@@ -361,7 +373,7 @@
         for line in range(lines):
             features[step, :, line * depth : (line + 1) * depth] = stage[line].astype(BF16)
         inputs = features[step]
-        hidden_one = jnp.tanh(mm(w_one[...].astype(BF16), inputs)).astype(BF16)
+        hidden_one = jnp.tanh(mm(w_one[...], inputs)).astype(BF16)
         one[step] = hidden_one
         hidden_two = jnp.tanh(mm(weight_mid[...], hidden_one) + b_mid[...]).astype(BF16)
         two[step] = hidden_two
@@ -460,10 +472,10 @@
         back = dot_full(out_x[...], spectrum)
         if number > 0:
             sent(2 * number - 1)
+        arrived = recv_b.at[number]
         for block in range(n_gy):
             part = dot_full(back, out_y[:, block * depth : (block + 1) * depth])
             send_b[block * n_gx : (block + 1) * n_gx] = part.reshape(n_gx, ROWS, depth)
-        arrived = recv_b.at[number]
         exchange(2 * number + 1, send_b, arrived)
         for part in range(pext.shape[0] // modes):
             pieces = [
@@ -509,33 +521,64 @@
     g_mid[...] = jnp.zeros_like(g_mid)
     g_out[...] = jnp.zeros_like(g_out)
     g_in[...] = jnp.zeros_like(g_in)
+    g_bias[...] = jnp.zeros_like(g_bias)
+
+    share = 2 * CHANNELS
+    packed = depth // share
+    own_lane = lax.broadcasted_iota(jnp.int32, (depth, depth), 1) // share
 
     def backward(step, carry):
         base = step * STEP
         for component in range(3):
             forces[:, component, :] = field[component, pl.ds(base, STEP)].reshape(lines, depth)
-        force = jnp.concatenate([forces[line].astype(BF16) for line in range(lines)], 1)
+        parts = []
+        for first in range(0, lines, packed):
+            rows = []
+            for line in range(first, first + packed):
+                parts.append(forces[line].astype(BF16))
+                rows.append(forces[line])
+                rows.append(features[step, :, line * depth : (line + 1) * depth].astype(F32))
+            turned = jnp.concatenate(rows, 0).T
+            for place in range(packed):
+                line = first + place
+                columns[line * depth : (line + 1) * depth, :] = jnp.where(
+                    own_lane == place, turned, 0.0
+                ).astype(BF16)
+        force = jnp.concatenate(parts, 1)
         hidden_two = two[step]
         hidden_one = one[step]
         value = hidden_two.astype(F32)
         delta_two = (mm(w_out_back[...], force) * (1.0 - value * value)).astype(BF16)
-        g_out[...] = g_out[...] + mm_cells(force, hidden_two)
-        g_mid[0:units, :] = g_mid[0:units, :] + mm_cells(hidden_one, delta_two)
-        g_mid[units:, :] = g_mid[units:, :] + mm_cells(force, delta_two)
+        g_out[...] = g_out[...] + mm(hidden_two, columns[...])
+        g_mid[...] = g_mid[...] + mm_cells(hidden_one, delta_two)
+        tall = g_bias[...]
+        for line in range(lines):
+            tall = tall + delta_two[:, line * depth : (line + 1) * depth].astype(F32)
+        g_bias[...] = tall
         value = hidden_one.astype(F32)
         delta_one = (mm(w_mid_back[...], delta_two) * (1.0 - value * value)).astype(BF16)
-        g_in[...] = g_in[...] + mm_cells(features[step], delta_one)
+        g_in[...] = g_in[...] + mm(delta_one, columns[...])
         return carry
 
     lax.fori_loop(0, steps, backward, 0)
 
     sent(2)
+    def folded(sums):
+        rows = sums.T
+        total = rows[0:share]
+        for place in range(1, packed):
+            total = total + rows[place * share : (place + 1) * share]
+        return total
+
+    for_in = folded(g_in[...])[CHANNELS:share]
+    for_out = folded(g_out[...])[0:CHANNELS]
+    for_bias = jnp.sum(g_bias[...].T, 0, keepdims=True)
     for half in range(2):
         lanes = slice(half * 128, half * 128 + 128)
-        small[half * CHANNELS : (half + 1) * CHANNELS, :] = g_in[:, lanes]
-        small[32 + half : 33 + half, :] = g_mid[units + 3 : units + 4, lanes]
-        small[34 + 3 * half : 37 + 3 * half, :] = g_out[0:3, lanes]
-    middle = g_mid[0:units, :].T
+        small[half * CHANNELS : (half + 1) * CHANNELS, :] = for_in[:, lanes]
+        small[32 + half : 33 + half, :] = for_bias[:, lanes]
+        small[34 + 3 * half : 37 + 3 * half, :] = for_out[0:3, lanes]
+    middle = g_mid[...].T
     for owner in range(group):
         tile = middle[owner * 8 : (owner + 1) * 8, :]
         send_a[owner, 0:8, :] = tile[:, 0:128]
@@ -592,16 +635,25 @@
     for half in range(2):
         lanes = slice(half * 128, half * 128 + 128)
         block = scaled[half * CHANNELS : (half + 1) * CHANNELS, :]
-        tall = jnp.concatenate([block, jnp.zeros((128 - CHANNELS, 128), F32)], 0).T
-        step_in[lanes, :] = tall[:, 0:FEATS]
+        step_in[:, lanes] = block[0:FEATS, :]
         step_bin[0:1, lanes] = block[FEATS : FEATS + 1, :]
         step_bmid[0:1, lanes] = scaled[32 + half : 33 + half, :]
         step_out[:, lanes] = scaled[34 + 3 * half : 37 + 3 * half, :]
-    step_bout[...] = bout / scale_rms
+    diagonal = lax.broadcasted_iota(jnp.int32, (3, 128), 0) == lax.broadcasted_iota(
+        jnp.int32, (3, 128), 1
+    )
+    flat = jnp.sum(jnp.where(diagonal, bout / scale_rms, 0.0), 0, keepdims=True)
+    step_bout[...] = flat[:, 0:3]
     cells_all = 3 * n_case * group * span_x * span_y * depth
     loss_ref[...] = cost / cells_all
     sent(4)
     sent(5)
+
+
+def hand_over(*refs):
+    count = len(refs) // 2
+    for source, target in zip(refs[:count], refs[count:]):
+        target[...] = source[...]
 
 
 def on_device(
@@ -634,12 +686,12 @@
         out_shape=(
             jax.ShapeDtypeStruct(velocity.shape, BF16),
             jax.ShapeDtypeStruct((1, 1), F32),
-            jax.ShapeDtypeStruct((units, FEATS), F32),
+            jax.ShapeDtypeStruct((FEATS, units), F32),
             jax.ShapeDtypeStruct((1, units), F32),
             jax.ShapeDtypeStruct((units, units), F32),
             jax.ShapeDtypeStruct((1, units), F32),
             jax.ShapeDtypeStruct((3, units), F32),
-            jax.ShapeDtypeStruct((3, 1), F32),
+            jax.ShapeDtypeStruct((1, 3), F32),
             jax.ShapeDtypeStruct(velocity.shape, BF16),
         ),
         in_specs=[vmem] * 7 + [smem, vmem, vmem, smem, vmem] + [vmem] * len(tables),
@@ -657,15 +709,17 @@
             pltpu.VMEM((lines, CHANNELS, depth), F32),
             pltpu.VMEM((lines, CHANNELS, depth), F32),
             pltpu.VMEM((lines, 8, depth), F32),
-            pltpu.VMEM((units, CHANNELS), F32),
+            pltpu.VMEM((units, CHANNELS), BF16),
             pltpu.VMEM((CHANNELS, units), F32),
             pltpu.VMEM((units, units), BF16),
             pltpu.VMEM((units, CHANNELS), BF16),
             pltpu.VMEM((units, 1), F32),
             pltpu.VMEM((8, 128), F32),
-            pltpu.VMEM((units + CHANNELS, units), F32),
-            pltpu.VMEM((CHANNELS, units), F32),
-            pltpu.VMEM((CHANNELS, units), F32),
+            pltpu.VMEM((units, units), F32),
+            pltpu.VMEM((units, depth), F32),
+            pltpu.VMEM((units, depth), F32),
+            pltpu.VMEM((units, depth), F32),
+            pltpu.VMEM((wide, depth), BF16),
             pltpu.VMEM((2 * group, 128), F32),
             pltpu.VMEM((2, 3, span_x, depth), BF16),
             pltpu.VMEM((2, 3, span_y, depth), BF16),
@@ -694,7 +748,7 @@
     )(
         velocity,
         target,
-        weight_in,
+        weight_in.T,
         bias_in[None, :],
         weight_mid,
         bias_mid[None, :],
@@ -706,16 +760,24 @@
         tile_weight,
         *tables,
     )
+    outs = pl.pallas_call(
+        hand_over,
+        out_shape=tuple(jax.ShapeDtypeStruct(out.shape, out.dtype) for out in outs),
+        in_specs=[vmem] * len(outs),
+        out_specs=(vmem,) * len(outs),
+        compiler_params=pltpu.CompilerParams(vmem_limit_bytes=60 * 1024 * 1024),
+        name="hand_over",
+    )(*outs)
     new, loss, step_in, step_bin, step_mid, step_bmid, step_out, step_bout, force = outs
     return (
         new,
         loss[0, 0],
-        step_in,
+        step_in.T,
         step_bin[0],
         step_mid,
         step_bmid[0],
         step_out,
-        step_bout[:, 0],
+        step_bout[0],
         force,
     )
 

time: 123 us -> 110 us (0.89)
  local copies, waits for them, and re-layouts: 8.49 us -> 0 us
  between operations: 2.49 us -> 0.65 us
    unnamed x20 -> x0, local copies, waits for them, and re-layouts: 8.49 us -> none
    pallas_call x1, Pallas kernels: 111 us -> 107 us  [on_device(): pl.pallas_call(functools.partial(step_kernel, sizes), out_shape=(jax.Shap...]
    pallas_call x0 -> x1, Pallas kernels: none -> 2.67 us  [on_device(): pl.pallas_call(hand_over, out_shape=tuple((jax.ShapeDtypeStruct(out.shape...]
where the time goes in v3:
time: 110 us
  Pallas kernels  110 us (100%)
    pallas_call x1, Pallas kernels, on_device(): pl.pallas_call(functools.partial(step_kernel, sizes), out_shape=(jax.Shap...  107 us
    pallas_call x1, Pallas kernels, on_device(): pl.pallas_call(hand_over, out_shape=tuple((jax.ShapeDtypeStruct(out.shape...  2.67 us

profile of v3, /device:TPU:0, one launch (start us, length us, event | category | flops | bytes accessed | tf_op | source)
XLA Modules:
  0.0 110.2 jit_solution(964976825385765972)
XLA Ops:
  0.6 106.8 %flow_step.1 = (bf16[1,3,16,16,128]{4,3,2,1,0:T(8,128)(2,1)}, f32[1,1]{1,0:T(1,128)}, f32[12,256]{1,0:T(8,128)}, f32[1,256]{1,0:T(1,128)}, f32[256,256]{1,0:T(8,...) custom-call(bf16[1,3,16,16,128]{4,3,2,1,0:T(8,128)(2,1)} %v_ref.1, ...), custom_call_target="tpu_custom_call" | custom-call | tf_op jit(solution)/shard_map/flow_step/pallas_call | solution.py:684
  107.5 2.7 %hand_over.1 = (bf16[1,3,16,16,128]{4,3,2,1,0:T(8,128)(2,1)}, f32[1,1]{1,0:T(1,128)}, f32[12,256]{1,0:T(8,128)}, f32[1,256]{1,0:T(1,128)}, f32[256,256]{1,0:T(8,...) custom-call(bf16[1,3,16,16,128]{4,3,2,1,0:T(8,128)(2,1)} %get-tuple-element.2, ...), custom_call_target="tpu_custom_call" | custom-call | tf_op jit(solution)/shard_map/hand_over/pallas_call | solution.py:763

commit v4 on v3

--- a/solution.py
+++ b/solution.py
@@ -23,7 +23,7 @@
 LIVE = 18
 SLOTS = 32
 FIRST = 8
-STEP = 2
+STEP = 4
 CHANNELS = 16
 FEATS = 12
 

time: 110 us -> 110 us (level)
  no operation moved by 1% of the time
where the time goes in v4:
time: 110 us
  Pallas kernels  109 us (99%)
    pallas_call x1, Pallas kernels, on_device(): pl.pallas_call(functools.partial(step_kernel, sizes), out_shape=(jax.Shap...  106 us
    pallas_call x1, Pallas kernels, on_device(): pl.pallas_call(hand_over, out_shape=tuple((jax.ShapeDtypeStruct(out.shape...  2.67 us

profile of v4, /device:TPU:0, one launch (start us, length us, event | category | flops | bytes accessed | tf_op | source)
XLA Modules:
  0.0 109.6 jit_solution(3774257181621208377)
XLA Ops:
  0.6 106.3 %flow_step.1 = (bf16[1,3,16,16,128]{4,3,2,1,0:T(8,128)(2,1)}, f32[1,1]{1,0:T(1,128)}, f32[12,256]{1,0:T(8,128)}, f32[1,256]{1,0:T(1,128)}, f32[256,256]{1,0:T(8,...) custom-call(bf16[1,3,16,16,128]{4,3,2,1,0:T(8,128)(2,1)} %v_ref.1, ...), custom_call_target="tpu_custom_call" | custom-call | tf_op jit(solution)/shard_map/flow_step/pallas_call | solution.py:684
  106.9 2.7 %hand_over.1 = (bf16[1,3,16,16,128]{4,3,2,1,0:T(8,128)(2,1)}, f32[1,1]{1,0:T(1,128)}, f32[12,256]{1,0:T(8,128)}, f32[1,256]{1,0:T(1,128)}, f32[256,256]{1,0:T(8,...) custom-call(bf16[1,3,16,16,128]{4,3,2,1,0:T(8,128)(2,1)} %get-tuple-element.2, ...), custom_call_target="tpu_custom_call" | custom-call | tf_op jit(solution)/shard_map/hand_over/pallas_call | solution.py:763
